TPU v7x, 32 devices: a whole 2x2x4 slice. The times are simulated.
32 devices in a mesh: blk: 8 (over z, core), ctr: 4 (over y, x).
Axes of the slice: x: 2, y: 2, z: 4, core: 2. Of those that a mesh axis runs over, the one named last changes fastest.
Arguments:
- integrals: float32 [8, 3200, 12800], P('blk', None, 'ctr'), may hold values from -0.078125 to 0.078125
- amplitudes: float32 [8, 12800, 128], P(None, 'ctr', 'blk'), may hold values from -6 to 6
- blockmap: int32 [8], replicated, may hold values from 0 to 7, each once
- vir_energy: float32 [320], replicated, may hold values from 0.2 to 3
- occ_energy: float32 [32], replicated, may hold values from -2 to -0.3
Outputs:
- ladder: float32 [8, 3200, 128], P('blk', 'ctr')
- increment: float32 [8, 3200, 128], P('blk', 'ctr')
Inputs may be any that keep to these rules, and one draw needn't show every extreme that they name: `blockmap`: every block number appears in exactly one slot.
All inputs are finite; a program needn't handle non-finite values.
Results may differ from a plain program's by a relative error of at most 0.0003.
Values sent between devices are 32-bit elements; how exact they have to be, the bound alone decides.
No kernel may reach another device: no remote copies, remote signals or barrier semaphores. Data moves between devices by JAX's collectives and lax.ppermute only.
A program may use at most 128 MiB of HBM per device.

v0:
```python
import jax
import jax.numpy as jnp
from jax import lax
from jax.sharding import PartitionSpec as P

NIRR = 8
VI = 40
OI = 4


def denominator(block, groups, ab_block, start, count, columns, vir_energy, occ_energy):
    irrep = block // groups
    rows = block % groups * ab_block + start + jnp.arange(count, dtype=jnp.int32)
    arow = rows // (VI * VI)
    first = arow * VI + rows // VI % VI
    second = jnp.bitwise_xor(arow, irrep) * VI + rows % VI
    cols = jnp.arange(columns, dtype=jnp.int32)
    orow = cols // (OI * OI)
    hole_one = orow * OI + cols // OI % OI
    hole_two = jnp.bitwise_xor(orow, irrep) * OI + cols % OI
    upper = jnp.take(vir_energy, first) + jnp.take(vir_energy, second)
    lower = jnp.take(occ_energy, hole_one) + jnp.take(occ_energy, hole_two)
    return upper[:, None] - lower[None, :]


def on_device(integrals, amplitudes, blockmap, vir_energy, occ_energy):
    blocks = lax.axis_size("blk")
    groups = blocks // NIRR
    block = blockmap[lax.axis_index("blk")]
    irrep = block // groups
    local = integrals[0]
    ab_block = local.shape[0]
    share = ab_block // lax.axis_size("ctr")
    chosen = lax.dynamic_index_in_dim(
        lax.all_gather(amplitudes, "blk", axis=2, tiled=True), irrep, 0, keepdims=False
    )
    partial_value = jnp.dot(
        local, chosen, preferred_element_type=jnp.float32, precision=lax.Precision.HIGHEST
    )
    offset = lax.axis_index("ctr") * share
    summed = lax.psum(partial_value, "ctr")
    mine = lax.dynamic_slice_in_dim(summed, offset, share, 0)
    denom = denominator(
        block, groups, ab_block, offset, share, partial_value.shape[1], vir_energy, occ_energy
    )
    return (mine[None], (mine / denom)[None])


def solution(mesh):
    placed = (P("blk", None, "ctr"), P(None, "ctr", "blk"), P(), P(), P())
    return jax.shard_map(
        on_device,
        mesh=mesh,
        in_specs=placed,
        out_specs=(P("blk", "ctr", None), P("blk", "ctr", None)),
        check_vma=False,
    )
```

profile of v0, /device:TPU:0, one launch (start us, length us, event | category | flops | bytes accessed | tf_op | source)
XLA Modules:
  0.0 246.5 jit_solution(3683687384088820996)
XLA Ops:
  7.2 0.0 copy-start
  7.2 0.0 all-gather.2.cloned.1.call-start
  7.2 0.7 all-gather.2.cloned.1.call-update
  7.9 0.0 all-reduce.2.cloned.1.call-start
  8.0 1.2 dynamic_slice.10
  11.2 0.0 copy-start.1
  11.2 122.2 %all-gather.2.cloned.1.call-done = f32[8,3200,128]{1,2,0:T(8,128)} async-done(((f32[8,3200,16]{1,2,0:T(8,128)}), f32[8,3200,128]{1,2,0:T(8,128)}) %all-gather.2.cloned.1.call-update) | async-done | bytes 13107216 | tf_op jit(solution)/shard_map/all_gather | solution.py:35
  133.4 42.8 %fusion.2 = f32[3200,128]{0,1:T(8,128)} fusion(f32[1,3200,3200]{2,1,0:T(8,128)} %param.9, f32[8,3200,128]{1,2,0:T(8,128)} %all-gather.2.cloned.1.call-done, s32[]{:T(128)S(6)} %select_n.73), kind=kOutput, calls=%fused_computation.6 | convolution fusion | flops 15728640000 | bytes 44236804 | tf_op jit(solution)/shard_map/dot_general | solution.py:37
  176.2 0.0 all-reduce.2.cloned.1.call-update
  176.3 0.0 copy-done.1
  176.3 1.2 gather_fusion.2
  177.5 0.7 compare_select_fusion.2
  178.2 1.2 gather_fusion.3
  179.4 0.7 compare_select_fusion
  180.1 0.0 copy-done
  180.1 5.4 %gather_fusion.1 = f32[800]{0:T(1024)S(1)} fusion(f32[320]{0:T(512)S(1)} %copy-done, s32[1024]{0:T(1024)S(1)} %pad_clamp_fusion.2), kind=kCustom, calls=%fused_computation.2.clone | custom fusion | bytes 9600 | tf_op jit(solution)/shard_map/jit(_take)/gather | solution.py:21
  185.6 5.4 %gather_fusion = f32[800]{0:T(1024)S(1)} fusion(f32[320]{0:T(512)S(1)} %copy-done, s32[1024]{0:T(1024)S(1)} %pad_clamp_fusion.3), kind=kCustom, calls=%fused_computation.clone | custom fusion | bytes 9600 | tf_op jit(solution)/shard_map/jit(_take)/gather | solution.py:21
  191.1 0.7 fusion.17
  191.7 0.7 select_add_fusion
  192.4 44.2 %all-reduce.2.cloned.1.call-done = f32[3200,128]{0,1:T(8,128)} async-done(((f32[3200,128]{0,1:T(8,128)}), f32[3200,128]{0,1:T(8,128)}) %all-reduce.2.cloned.1.call-update) | async-done | bytes 1638416 | tf_op jit(solution)/shard_map/psum | solution.py:41
  236.6 1.2 divide_bitcast_fusion
  237.8 0.9 copy.9
  238.8 0.9 copy.8
  (6 shorter events, 0.1 us)
Async XLA Ops:
  7.2 173.0 %copy-start = (f32[320]{0:T(512)S(1)}, f32[320]{0:T(512)}, u32[]{:S(2)}) copy-start(f32[320]{0:T(512)} %param.12) | copy-start | bytes 3844
  7.2 126.2 %all-gather.2.cloned.1.call-start = ((), (), s32[]{:S(2)}) async-start(), calls=%async_computation | async-start | bytes 14745600 | tf_op jit(solution)/shard_map/all_gather | solution.py:35
  7.9 228.7 %all-reduce.2.cloned.1.call-start = ((), (), s32[]{:S(2)}) async-start(), calls=%async_computation.1 | async-start | bytes 3276800 | tf_op jit(solution)/shard_map/psum | solution.py:41
  11.2 165.1 %copy-start.1 = (f32[32]{0:T(128)S(1)}, f32[32]{0:T(128)}, u32[]{:S(2)}) copy-start(f32[32]{0:T(128)} %param.13) | copy-start | bytes 388
Sparse Core Ops, SparseCore 0:
  9.6 123.7 all-gather.1
  176.4 60.1 all-reduce.1
where the time goes:
time: 247 us
  waiting for transfers between devices  167 us (68%)
  matrix products  42.8 us (17%)
  local copies, waits for them, and re-layouts  16.5 us (7%)
  between operations  16.1 us (7%)
  other arithmetic  3.97 us (2%)
    all_gather x1, waiting for transfers between devices, on_device(): lax.all_gather(amplitudes, 'blk', axis=2, tiled=True)  122 us
    psum x1, waiting for transfers between devices, on_device(): summed = lax.psum(partial_value, 'ctr')  44.2 us
    dot_general x1, matrix products, on_device(): jnp.dot(local, chosen, preferred_element_type=jnp.float32, precision=lax....  42.8 us
    gather x2, local copies, waits for them, and re-layouts, denominator(): upper = jnp.take(vir_energy, first) + jnp.take(vir_energy, second)  10.9 us
  transfers between devices with their start and end apart: 2, of which 2 were waited for; matrix products, arithmetic and copies ran while one was open for 7% of the time, Pallas kernels for 0%

commit v1 on v0

v1 whole, which is shorter than its diff:
```python
import functools

import jax
import jax.numpy as jnp
from jax import lax
from jax.experimental import pallas as pl
from jax.experimental.pallas import tpu as pltpu
from jax.sharding import PartitionSpec as P

NIRR = 8
VI = 40
OI = 4
F32 = jnp.float32
BF16 = jnp.bfloat16
ANY = pl.BlockSpec(memory_space=pl.ANY)
PREP_MIB = 4
NEAR_MIB = 9
FAR_MIB = 6
SMEM = pl.BlockSpec(memory_space=pltpu.SMEM)
HBM = pl.BlockSpec(memory_space=pltpu.HBM)
VMEM = pl.BlockSpec(memory_space=pltpu.VMEM)
NEAR = (0, 1, 2, 3)
FAR = (4, 5, 6, 7)
RING = 2


def cost(flops, nbytes):
    return pl.CostEstimate(flops=1, bytes_accessed=1, transcendentals=0)


def params(mib):
    return pltpu.CompilerParams(vmem_limit_bytes=mib * 1024 * 1024)


def denominator(block, groups, ab_block, start, count, columns, vir_energy, occ_energy):
    irrep = block // groups
    rows = block % groups * ab_block + start + jnp.arange(count, dtype=jnp.int32)
    arow = rows // (VI * VI)
    first = arow * VI + rows // VI % VI
    second = jnp.bitwise_xor(arow, irrep) * VI + rows % VI
    cols = jnp.arange(columns, dtype=jnp.int32)
    orow = cols // (OI * OI)
    hole_one = orow * OI + cols // OI % OI
    hole_two = jnp.bitwise_xor(orow, irrep) * OI + cols % OI
    upper = jnp.take(vir_energy, first) + jnp.take(vir_energy, second)
    lower = jnp.take(occ_energy, hole_one) + jnp.take(occ_energy, hole_two)
    return upper[:, None] - lower[None, :]


def general(integrals, amplitudes, blockmap, vir_energy, occ_energy):
    blocks = lax.axis_size("blk")
    groups = blocks // NIRR
    block = blockmap[lax.axis_index("blk")]
    local = integrals[0]
    ab_block = local.shape[0]
    share = ab_block // lax.axis_size("ctr")
    wanted = jnp.take(amplitudes, blockmap // groups, axis=0)
    parts = lax.all_to_all(wanted, "blk", 0, 0)
    chosen = jnp.moveaxis(parts, 0, 1).reshape(parts.shape[1], -1)
    partial_value = jnp.dot(local, chosen, preferred_element_type=F32, precision=lax.Precision.HIGHEST)
    mine = lax.psum_scatter(partial_value, "ctr", scatter_dimension=0, tiled=True)
    offset = lax.axis_index("ctr") * share
    denom = denominator(block, groups, ab_block, offset, share, mine.shape[1], vir_energy, occ_energy)
    return (mine[None], (mine / denom)[None])


def prep_kernel(messages, bm, amps, *refs):
    outs, sem = refs[:-1], refs[-1]
    me = lax.axis_index("blk")
    copies = [
        pltpu.make_async_copy(amps.at[bm[jnp.bitwise_xor(me, s)], :, pl.ds(k0, kc)], out, sem.at[n])
        for n, ((s, k0, kc), out) in enumerate(zip(messages, outs))
    ]
    for c in copies:
        c.start()
    for c in copies:
        c.wait()


def prep(blockmap, amps, messages):
    return pl.pallas_call(
        functools.partial(prep_kernel, messages),
        out_shape=[jax.ShapeDtypeStruct((amps.shape[1], kc), F32) for _, _, kc in messages],
        in_specs=[SMEM, HBM],
        out_specs=[VMEM] * len(messages),
        scratch_shapes=[pltpu.SemaphoreType.DMA((len(messages),))],
        compiler_params=params(PREP_MIB),
        cost_estimate=cost(0, 2 * 4 * amps.size),
        name="prep",
    )(blockmap, amps)


def split(x):
    hi = x.astype(BF16)
    return hi, (x - hi.astype(F32)).astype(BF16)


def weights(pieces, partners, starts, kc):
    me = lax.axis_index("blk")
    slot = [jnp.bitwise_and(jnp.bitwise_xor(me, s), 3) for s in partners]
    rows = []
    for q in range(4):
        held = [piece[:, k : k + kc] for piece, k in zip(pieces, starts)]
        x = held[3]
        for n in range(3):
            x = jnp.where(slot[n] == q, held[n], x)
        rows.append(x)
    hi, lo = split(jnp.concatenate(rows, 0).T)
    return jnp.concatenate([hi, lo], 1)


def fold(wide):
    value = wide + pltpu.roll(wide, 64, 1)
    half = value.shape[0] // 2
    left = lax.broadcasted_iota(jnp.int32, (half, 128), 1) < 64
    return jnp.where(left, value[:half], value[half:])


def near_kernel(k0, kc, starts, last, with_old, a, *refs):
    refs = list(refs)
    pieces = [refs.pop(0) for _ in NEAR]
    old = refs.pop(0) if with_old else None
    his, los = refs.pop(0), refs.pop(0)
    outs = [refs.pop(0) for _ in range(4 if last else 1)]
    buf, w, acc, sem = refs
    ctr = lax.axis_index("ctr")
    share = a.shape[0] // 4

    def load(n):
        return pltpu.make_async_copy(
            a.at[pl.ds(n * share, share), pl.ds(k0, kc)], buf.at[lax.rem(n, RING)], sem.at[lax.rem(n, RING)]
        )

    for n in range(RING):
        load(n).start()
    w[...] = weights(pieces, NEAR, starts, kc)
    sums = acc if last else outs[0]

    @pl.loop(0, 4)
    def _(t):
        load(t).wait()
        at = pl.ds(t * share, share)
        hi, lo = split(buf[lax.rem(t, RING)])
        his[at, :] = hi
        los[at, :] = lo

        @pl.when(t + RING < 4)
        def _():
            load(t + RING).start()

        wide = jnp.dot(his[at, :], w[...], preferred_element_type=F32)
        x = fold(wide + jnp.dot(los[at, :], w[...], preferred_element_type=F32))
        sums[t] = x + old[t] if with_old else x

    if last:
        for s in range(4):
            outs[s][...] = acc[jnp.bitwise_xor(ctr, s)]


def near_tile(a, span, pieces, old, last):
    k0, kc = span
    starts = [k0 - held for held, _ in pieces]
    rows = a.shape[0]
    kept = jax.ShapeDtypeStruct((rows, kc), BF16)
    packed = (rows // 8, 128)
    given = [x for _, x in pieces] + ([old] if old is not None else [])
    sums = [jax.ShapeDtypeStruct(packed, F32)] * 4 if last else [jax.ShapeDtypeStruct((4, *packed), F32)]
    out = pl.pallas_call(
        functools.partial(near_kernel, k0, kc, starts, last, old is not None),
        out_shape=[kept, kept, *sums],
        in_specs=[ANY] + [VMEM] * len(given),
        out_specs=[VMEM] * (2 + len(sums)),
        scratch_shapes=[
            pltpu.VMEM((RING, rows // 4, kc), F32),
            pltpu.VMEM((kc, 128), BF16),
            pltpu.VMEM((4, *packed), F32),
            pltpu.SemaphoreType.DMA((RING,)),
        ],
        compiler_params=params(NEAR_MIB),
        cost_estimate=cost(2 * 2 * rows * kc * 256, 4 * rows * kc),
        name="near",
    )(a, *given)
    return out[:2], (out[2:] if last else out[2])


def far_kernel(spans, s, first, *refs):
    refs = list(refs)
    kept = [(refs.pop(0), refs.pop(0)) for _ in spans]
    if first:
        pieces = [refs.pop(0) for _ in FAR]
        out, w = refs
        for k0, kc in spans:
            w[k0 : k0 + kc, :] = weights(pieces, FAR, [k0] * 4, kc)
    else:
        w, out = refs
    share = out.shape[0] * 2
    at = pl.ds(pl.multiple_of(jnp.bitwise_xor(lax.axis_index("ctr"), s) * share, share), share)
    wide = jnp.zeros((share, 128), F32)
    for (k0, kc), (hi, lo) in zip(spans, kept):
        part = w[k0 : k0 + kc, :]
        wide = wide + jnp.dot(hi[at, :], part, preferred_element_type=F32)
        wide = wide + jnp.dot(lo[at, :], part, preferred_element_type=F32)
    out[...] = fold(wide)


def far_tile(spans, kept, s, pieces=None, w=None):
    rows = kept[0][0].shape[0]
    cd = sum(kc for _, kc in spans)
    given = [x for pair in kept for x in pair] + ([w] if pieces is None else [*pieces])
    out = [jax.ShapeDtypeStruct((rows // 8, 128), F32)]
    if pieces is not None:
        out.append(jax.ShapeDtypeStruct((cd, 128), BF16))
    return pl.pallas_call(
        functools.partial(far_kernel, spans, s, pieces is not None),
        out_shape=out,
        in_specs=[VMEM] * len(given),
        out_specs=[VMEM] * len(out),
        compiler_params=params(FAR_MIB),
        cost_estimate=cost(2 * 2 * rows // 4 * cd * 256, 4 * rows // 4 * cd),
        name="far",
    )(*given)

def denom_kernel(count, bm, vir, occ, out):
    irrep = bm[lax.axis_index("blk")]
    start = lax.axis_index("ctr") * count
    vir_at = lax.broadcasted_iota(jnp.int32, (count, vir.shape[1]), 1)
    rows = start + lax.broadcasted_iota(jnp.int32, (count, vir.shape[1]), 0)
    arow = rows // (VI * VI)
    first = arow * VI + rows // VI % VI
    second = jnp.bitwise_xor(arow, irrep) * VI + rows % VI
    energy = jnp.broadcast_to(vir[...], vir_at.shape)
    pick = lambda at: jnp.sum(jnp.where(vir_at == at, energy, 0.0), axis=1, keepdims=True)
    upper = pick(first) + pick(second)
    occ_at = lax.broadcasted_iota(jnp.int32, (occ.shape[0], 128), 0)
    cols = lax.broadcasted_iota(jnp.int32, (occ.shape[0], 128), 1)
    orow = cols // (OI * OI)
    hole_one = orow * OI + cols // OI % OI
    hole_two = jnp.bitwise_xor(orow, irrep) * OI + cols % OI
    level = jnp.broadcast_to(occ[...], occ_at.shape)
    find = lambda at: jnp.sum(jnp.where(occ_at == at, level, 0.0), axis=0, keepdims=True)
    lower = find(hole_one) + find(hole_two)
    out[...] = upper - lower


def denominators(blockmap, vir_energy, occ_energy, count):
    return pl.pallas_call(
        functools.partial(denom_kernel, count),
        out_shape=jax.ShapeDtypeStruct((count, 128), F32),
        in_specs=[SMEM, VMEM, VMEM],
        out_specs=VMEM,
        compiler_params=params(8),
        cost_estimate=cost(count * 320 * 8, count * 128 * 4),
        name="denominators",
    )(blockmap, vir_energy.reshape(1, -1), occ_energy.reshape(-1, 1))


def add_kernel(*refs):
    refs[4][...] = (refs[0][...] + refs[1][...]) + (refs[2][...] + refs[3][...])


def add(parts):
    x = parts[0]
    return pl.pallas_call(
        add_kernel,
        out_shape=jax.ShapeDtypeStruct(x.shape, F32),
        in_specs=[VMEM] * 4,
        out_specs=VMEM,
        compiler_params=params(8),
        cost_estimate=cost(4 * x.size, 20 * x.size),
        name="add",
    )(*parts)


def finish_kernel(near, *refs):
    far, denom, ladder, inc = refs[:4], *refs[4:]
    low = lax.axis_index("blk") // 4 == 0
    near = near[...]
    far = (far[0][...] + far[1][...]) + (far[2][...] + far[3][...])
    one, two = jnp.where(low, near, far), jnp.where(low, far, near)
    rows = near.shape[0]
    left = lax.broadcasted_iota(jnp.int32, (rows, 128), 1) < 64
    values = (jnp.where(left, one, pltpu.roll(two, 64, 1)), jnp.where(left, pltpu.roll(one, 64, 1), two))
    for n, value in enumerate(values):
        at = slice(n * rows, (n + 1) * rows)
        ladder[0, at] = value
        inc[0, at] = value / denom[at]


def finish(near, far, denom):
    out = jax.ShapeDtypeStruct((1, *denom.shape), F32)
    return pl.pallas_call(
        finish_kernel,
        out_shape=[out, out],
        in_specs=[VMEM] * 6,
        out_specs=[VMEM] * 2,
        compiler_params=params(8),
        cost_estimate=cost(denom.size * 8, denom.size * 4 * 7),
        name="finish",
    )(near, *far, denom)


def swap(x, axis, s):
    n = lax.axis_size(axis)
    return lax.ppermute(x, axis, [(i, i ^ s) for i in range(n)])


def after(x, *first):
    return lax.optimization_barrier((x, *first))[0]


def ranges(total, parts):
    tiles = total // 128
    edges = [n * tiles // parts * 128 for n in range(parts + 1)]
    return [(a, b - a) for a, b in zip(edges, edges[1:])]


def special(integrals, amplitudes, blockmap, vir_energy, occ_energy):
    a = integrals[0]
    amps = jnp.swapaxes(amplitudes, 1, 2)
    spans = ranges(amps.shape[2], 4)
    cd = amps.shape[2]
    cut = spans[2][0]
    halves = ((0, cut), (cut, cd - cut))
    messages = [(0, 0, cd), (1, 0, cd)] + [(s, *half) for half in halves for s in (2, 3)] + [(s, 0, cd) for s in FAR]
    sends = prep(blockmap, amps, messages)
    denom = denominators(blockmap, vir_energy, occ_energy, a.shape[0] // 4)
    here = [(0, sends[0]), (0, swap(sends[1], "blk", 1))]
    early = [swap(x, "blk", s) for s, x in zip((2, 3), sends[2:4])]
    late = [swap(after(x, denom, *early), "blk", s) for s, x in zip((2, 3), sends[4:6])]
    far = [swap(x, "blk", s) for s, x in zip(FAR, sends[6:10])]
    kept, sums = [], None
    for n, span in enumerate(spans):
        rest = [(0, x) for x in early] if n < 2 else [(cut, x) for x in late]
        pair, sums = near_tile(a, span, here + rest, sums, n == len(spans) - 1)
        kept.append(pair)
    near_sum = add([sums[0], *[swap(sums[s], "ctr", s) for s in (1, 2, 3)]])
    first, w = far_tile(spans, kept, 3, far)
    far_sums = {3: swap(first, "ctr", 3)}
    for s in (1, 2, 0):
        x = far_tile(spans, kept, s, None, w if s else after(w, near_sum))[0]
        far_sums[s] = swap(x, "ctr", s) if s else x
    return tuple(finish(near_sum, [far_sums[s] for s in range(4)], denom))


def on_device(integrals, amplitudes, *rest):
    _, rows, cd = integrals.shape
    fits = (
        lax.axis_size("blk") == NIRR
        and lax.axis_size("ctr") == 4
        and rows % 128 == 0
        and cd % 128 == 0
        and amplitudes.shape[2] == 16
    )
    return (special if fits else general)(integrals, amplitudes, *rest)


def solution(mesh):
    placed = (P("blk", None, "ctr"), P(None, "ctr", "blk"), P(), P(), P())
    return jax.shard_map(
        on_device,
        mesh=mesh,
        in_specs=placed,
        out_specs=(P("blk", "ctr", None), P("blk", "ctr", None)),
        check_vma=False,
    )
```

time: 247 us -> 78.6 us (0.32)
  waiting for transfers between devices: 167 us -> 7.97 us
  Pallas kernels: 0 us -> 45 us
  matrix products: 42.8 us -> 0 us
  starting transfers between devices: 0.08 us -> 19.8 us
  between operations: 16.1 us -> 0.77 us
  local copies, waits for them, and re-layouts: 16.5 us -> 4.16 us
  other arithmetic: 3.97 us -> 0 us
    all_gather x1 -> x0, waiting for transfers between devices: 122 us -> none  [on_device(): lax.all_gather(amplitudes, 'blk', axis=2, tiled=True)]
    pallas_call x0 -> x12, Pallas kernels: none -> 45 us  [the longest x4 27.3 us: near_tile(): pl.pallas_call(functools.partial(near_kernel, k0, kc, starts, last, old i...]
    psum x1 -> x0, waiting for transfers between devices: 44.2 us -> none  [on_device(): summed = lax.psum(partial_value, 'ctr')]
    dot_general x1 -> x0, matrix products: 42.8 us -> none  [on_device(): jnp.dot(local, chosen, preferred_element_type=jnp.float32, precision=lax....]
    ppermute x0 -> x15, starting transfers between devices: none -> 19.8 us  [swap(): return lax.ppermute(x, axis, [(i, i ^ s) for i in range(n)])]
    gather x4 -> x0, local copies, waits for them, and re-layouts: 13.3 us -> none  [the longest x2 10.9 us: denominator(): upper = jnp.take(vir_energy, first) + jnp.take(vir_energy, second)]
    ppermute x0 -> x15, waiting for transfers between devices: none -> 7.97 us  [swap(): return lax.ppermute(x, axis, [(i, i ^ s) for i in range(n)])]
  transfers between devices with their start and end apart: 2 -> 15, of which waited for: 2 -> 5; matrix products, arithmetic and copies ran while one was open for 7% -> 2% of each run, Pallas kernels for 0% -> 53%
where the time goes in v1:
time: 78.6 us; the launch traced here: 77.7 us
  Pallas kernels  45 us (57%)
  starting transfers between devices  19.8 us (25%)
  waiting for transfers between devices  7.97 us (10%)
  local copies, waits for them, and re-layouts  4.16 us (5%)
    pallas_call x4, Pallas kernels, near_tile(): pl.pallas_call(functools.partial(near_kernel, k0, kc, starts, last, old i...  27.3 us
    ppermute x15, starting transfers between devices, swap(): return lax.ppermute(x, axis, [(i, i ^ s) for i in range(n)])  19.8 us
    pallas_call x4, Pallas kernels, far_tile(): pl.pallas_call(functools.partial(far_kernel, spans, s, pieces is not None...  12.2 us
    ppermute x15, waiting for transfers between devices, swap(): return lax.ppermute(x, axis, [(i, i ^ s) for i in range(n)])  7.97 us
    unnamed x10, local copies, waits for them, and re-layouts  2.74 us
    pallas_call x1, Pallas kernels, prep(): pl.pallas_call(functools.partial(prep_kernel, messages), out_shape=[jax.S...  2.61 us
    pallas_call x1, Pallas kernels, denominators(): pl.pallas_call(functools.partial(denom_kernel, count), out_shape=jax.Shap...  1.72 us
  transfers between devices with their start and end apart: 15, of which 5 were waited for; matrix products, arithmetic and copies ran while one was open for 2% of the time, Pallas kernels for 53%

profile of v1, /device:TPU:0, one launch (start us, length us, event | category | flops | bytes accessed | tf_op | source)
XLA Modules:
  0.0 77.7 jit_solution(2945439423059838033)
XLA Ops:
  0.6 1.4 %copy-done.2 = f32[8,3200,16]{1,2,0:T(8,128)S(1)} copy-done((f32[8,3200,16]{1,2,0:T(8,128)S(1)}, f32[8,3200,16]{1,2,0:T(8,128)}, u32[]{:S(2)}) %copy-start.2) | copy-done | bytes 1638424
  2.1 0.7 copy-done.3
  2.7 2.6 %prep.1 = (f32[16,3200]{1,0:T(8,128)S(1)}, f32[16,3200]{1,0:T(8,128)S(1)}, f32[16,1536]{1,0:T(8,128)S(1)}, f32[16,1536]{1,0:T(8,128)S(1)}, f32[16,1664]{1,0:T(8,...) custom-call(s32[8]{0:T(128)S(1)} %copy-done.3, ...), custom_call_target="tpu_custom_call" | custom-call | flops 1 | bytes 1 | tf_op jit(solution)/shard_map/prep/pallas_call | solution.py:81
  5.3 3.1 %collective-permute-start.1 = (f32[16,1536]{1,0:T(8,128)S(1)}, f32[16,1536]{1,0:T(8,128)S(1)}, u32[]{:S(2)}, u32[]{:S(2)}) collective-permute-start(f32[16,1536]{1,0:T(8,128)S(1)} %get-tuple-element.35), channel_id=1, source_target_pairs={{0,8},{4,12},{8,0},{12,4},{16,24},{20,28},{24,16},{28,20},{1,9},{5... | collective-permute-start | bytes 294920 | tf_op jit(solution)/shard_map/ppermute | solution.py:304
  8.6 0.7 reshape.10.vir
  9.3 0.7 copy.7.occ
  10.0 0.7 copy-done.4
  10.7 1.7 %denominators.1.refs_4_ = f32[800,128]{1,0:T(8,128)S(1)} custom-call(s32[8]{0:T(128)S(1)} %copy-done.4, f32[1,320]{1,0:T(1,128)S(1)} %reshape.10.vir, f32[32,1]{1,0:T(8,128)S(1)} %copy.7.occ), custom_call_target="tpu_custom_call" | custom-call | flops 1 | bytes 1 | tf_op jit(solution)/shard_map/denominators/pallas_call | solution.py:246
  12.4 0.9 %collective-permute-done.2.refs_3_ = f32[16,1536]{1,0:T(8,128)S(1)} collective-permute-done((f32[16,1536]{1,0:T(8,128)S(1)}, f32[16,1536]{1,0:T(8,128)S(1)}, u32[]{:S(2)}, u32[]{:S(2)}) %collective-permute-start.2) | collective-permute-done | bytes 98336 | tf_op jit(solution)/shard_map/ppermute | solution.py:304
  13.3 1.1 %collective-permute-start.3 = (f32[16,1664]{1,0:T(8,128)S(1)}, f32[16,1664]{1,0:T(8,128)S(1)}, u32[]{:S(2)}, u32[]{:S(2)}) collective-permute-start(f32[16,1664]{1,0:T(8,128)S(1)} %get-tuple-element.37), channel_id=1, source_target_pairs={{0,8},{4,12},{8,0},{12,4},{16,24},{20,28},{24,16},{28,20},{1,9},{5... | collective-permute-start | bytes 319496 | tf_op jit(solution)/shard_map/ppermute | solution.py:304
  14.5 3.0 %collective-permute-start.8 = (f32[16,3200]{1,0:T(8,128)S(1)}, f32[16,3200]{1,0:T(8,128)S(1)}, u32[]{:S(2)}, u32[]{:S(2)}) collective-permute-start(f32[16,3200]{1,0:T(8,128)S(1)} %get-tuple-element.55), channel_id=1, source_target_pairs={{0,16},{4,20},{8,24},{12,28},{16,0},{20,4},{24,8},{28,12},{1,17},{... | collective-permute-start | bytes 614408 | tf_op jit(solution)/shard_map/ppermute | solution.py:304
  17.6 0.3 collective-permute-start.9
  17.9 0.9 %collective-permute-done.3.refs_2_ = f32[16,1664]{1,0:T(8,128)S(1)} collective-permute-done((f32[16,1664]{1,0:T(8,128)S(1)}, f32[16,1664]{1,0:T(8,128)S(1)}, u32[]{:S(2)}, u32[]{:S(2)}) %collective-permute-start.3) | collective-permute-done | bytes 106528 | tf_op jit(solution)/shard_map/ppermute | solution.py:304
  18.7 4.8 %collective-permute-start.10 = (f32[16,3200]{1,0:T(8,128)S(1)}, f32[16,3200]{1,0:T(8,128)S(1)}, u32[]{:S(2)}, u32[]{:S(2)}) collective-permute-start(f32[16,3200]{1,0:T(8,128)S(1)} %get-tuple-element.57), channel_id=1, source_target_pairs={{0,24},{4,28},{8,16},{12,20},{16,8},{20,12},{24,0},{28,4},{1,25},{... | collective-permute-start | bytes 614408 | tf_op jit(solution)/shard_map/ppermute | solution.py:304
  23.6 6.0 %near.4 = (bf16[3200,768]{1,0:T(8,128)(2,1)S(1)}, bf16[3200,768]{1,0:T(8,128)(2,1)S(1)}, f32[4,400,128]{2,1,0:T(8,128)S(1)}) custom-call(f32[3200,3200]{1,0:T(8,128)} %bitcast.4, f32[16,3200]{1,0:T(8,128)S(1)} %get-tuple-element.32.refs_0_, f32[16,3200]{1,0:T(8,128)S(1)} %collective-permute-done.refs_1_, f32[16,1536]{1,0:T(8,128)S(1)} %collective-permute-done.1.refs_2_, ...), custom_call_target="tpu_custom_call" | custom-call | flops 1 | bytes 1 | tf_op jit(solution)/shard_map/near/pallas_call | solution.py:168
  29.6 6.2 %near.5 = (bf16[3200,768]{1,0:T(8,128)(2,1)S(1)}, bf16[3200,768]{1,0:T(8,128)(2,1)S(1)}, f32[4,400,128]{2,1,0:T(8,128)S(1)}) custom-call(f32[3200,3200]{1,0:T(8,128)} %bitcast.5, f32[16,3200]{1,0:T(8,128)S(1)} %get-tuple-element.32.refs_0_, f32[16,3200]{1,0:T(8,128)S(1)} %collective-permute-done.refs_1_, f32[16,1536]{1,0:T(8,128)S(1)} %collective-permute-done.1.refs_2_, ...), custom_call_target="tpu_custom_call" | custom-call | flops 1 | bytes 1 | tf_op jit(solution)/shard_map/near/pallas_call | solution.py:168
  35.9 8.0 %near.6 = (bf16[3200,768]{1,0:T(8,128)(2,1)S(1)}, bf16[3200,768]{1,0:T(8,128)(2,1)S(1)}, f32[4,400,128]{2,1,0:T(8,128)S(1)}) custom-call(f32[3200,3200]{1,0:T(8,128)} %bitcast.6, f32[16,3200]{1,0:T(8,128)S(1)} %get-tuple-element.32.refs_0_, f32[16,3200]{1,0:T(8,128)S(1)} %collective-permute-done.refs_1_, f32[16,1664]{1,0:T(8,128)S(1)} %collective-permute-done.3.refs_2_, ...), custom_call_target="tpu_custom_call" | custom-call | flops 1 | bytes 1 | tf_op jit(solution)/shard_map/near/pallas_call | solution.py:168
  43.9 7.1 %near.7 = (bf16[3200,896]{1,0:T(8,128)(2,1)S(1)}, bf16[3200,896]{1,0:T(8,128)(2,1)S(1)}, f32[400,128]{1,0:T(8,128)S(1)}, f32[400,128]{1,0:T(8,128)S(1)}, f32[400,128]{1,0:T(8,128)S(1)}, /*index=5*/f32[400,128]{1,0:T(8,128)S(1)}) custom-call(f32[3200,3200]{1,0:T(8,128)} %bitcast.7, f32[16,3200]{1,0:T(8,128)S(1)} %get-tuple-element.32.refs_0_, ...), custom_call_target="tpu_custom_call" | custom-call | flops 1 | bytes 1 | tf_op jit(solution)/shard_map/near/pallas_call | solution.py:168
  51.0 1.6 %collective-permute-start.5 = (f32[400,128]{1,0:T(8,128)S(1)}, f32[400,128]{1,0:T(8,128)S(1)}, u32[]{:S(2)}, u32[]{:S(2)}) collective-permute-start(f32[400,128]{1,0:T(8,128)S(1)} %get-tuple-element.44), channel_id=1, source_target_pairs={{0,1},{1,0},{2,3},{3,2},{4,5},{5,4},{6,7},{7,6},{8,9},{9,8},{10,11... | collective-permute-start | bytes 614408 | tf_op jit(solution)/shard_map/ppermute | solution.py:304
  52.6 1.5 %collective-permute-start.6 = (f32[400,128]{1,0:T(8,128)S(1)}, f32[400,128]{1,0:T(8,128)S(1)}, u32[]{:S(2)}, u32[]{:S(2)}) collective-permute-start(f32[400,128]{1,0:T(8,128)S(1)} %get-tuple-element.45), channel_id=1, source_target_pairs={{0,2},{1,3},{2,0},{3,1},{4,6},{5,7},{6,4},{7,5},{8,10},{9,11},{10,... | collective-permute-start | bytes 614408 | tf_op jit(solution)/shard_map/ppermute | solution.py:304
  54.1 0.5 collective-permute-start.7
  54.6 3.4 %far.4 = (f32[400,128]{1,0:T(8,128)S(1)}, bf16[3200,128]{1,0:T(8,128)(2,1)S(1)}) custom-call(bf16[3200,768]{1,0:T(8,128)(2,1)S(1)} %get-tuple-element.47.refs_0_, bf16[3200,768]{1,0:T(8,128)(2,1)S(1)} %get-tuple-element.48.refs_1_, bf16[3200,768]{1,0:T(8,128)(2,1)S(1)} %get-tuple-element.49.refs_2_, bf16[3200,768]{1,0:T(8,128)(2,1)S(1)} %copy-done.1, ...), custom_call_target="tpu_custom_call" | custom-call | flops 1 | bytes 1 | tf_op jit(solution)/shard_map/far/pallas_call | solution.py:213
  58.0 2.9 %far.7 = f32[400,128]{1,0:T(8,128)S(1)} custom-call(bf16[3200,768]{1,0:T(8,128)(2,1)S(1)} %get-tuple-element.47.refs_0_, bf16[3200,768]{1,0:T(8,128)(2,1)S(1)} %get-tuple-element.48.refs_1_, bf16[3200,768]{1,0:T(8,128)(2,1)S(1)} %get-tuple-element.49.refs_2_, bf16[3200,768]{1,0:T(8,128)(2,1)S(1)} %copy-done.1, ...), custom_call_target="tpu_custom_call" | custom-call | flops 1 | bytes 1 | tf_op jit(solution)/shard_map/far/pallas_call | solution.py:213
  60.9 2.9 %far.6 = f32[400,128]{1,0:T(8,128)S(1)} custom-call(bf16[3200,768]{1,0:T(8,128)(2,1)S(1)} %get-tuple-element.47.refs_0_, bf16[3200,768]{1,0:T(8,128)(2,1)S(1)} %get-tuple-element.48.refs_1_, bf16[3200,768]{1,0:T(8,128)(2,1)S(1)} %get-tuple-element.49.refs_2_, bf16[3200,768]{1,0:T(8,128)(2,1)S(1)} %copy-done.1, ...), custom_call_target="tpu_custom_call" | custom-call | flops 1 | bytes 1 | tf_op jit(solution)/shard_map/far/pallas_call | solution.py:213
  63.9 1.6 %collective-permute-start.12 = (f32[400,128]{1,0:T(8,128)S(1)}, f32[400,128]{1,0:T(8,128)S(1)}, u32[]{:S(2)}, u32[]{:S(2)}) collective-permute-start(f32[400,128]{1,0:T(8,128)S(1)} %far.6), channel_id=1, source_target_pairs={{0,1},{1,0},{2,3},{3,2},{4,5},{5,4},{6,7},{7,6},{8,9},{9,8},{10,11... | collective-permute-start | bytes 614408 | tf_op jit(solution)/shard_map/ppermute | solution.py:304
  65.5 1.5 %collective-permute-start.13 = (f32[400,128]{1,0:T(8,128)S(1)}, f32[400,128]{1,0:T(8,128)S(1)}, u32[]{:S(2)}, u32[]{:S(2)}) collective-permute-start(f32[400,128]{1,0:T(8,128)S(1)} %far.7), channel_id=1, source_target_pairs={{0,2},{1,3},{2,0},{3,1},{4,6},{5,7},{6,4},{7,5},{8,10},{9,11},{10,... | collective-permute-start | bytes 614408 | tf_op jit(solution)/shard_map/ppermute | solution.py:304
  67.0 0.5 collective-permute-start.14
  67.5 2.9 %far.5.refs_0_ = f32[400,128]{1,0:T(8,128)S(1)} custom-call(bf16[3200,768]{1,0:T(8,128)(2,1)S(1)} %get-tuple-element.47.refs_0_, bf16[3200,768]{1,0:T(8,128)(2,1)S(1)} %get-tuple-element.48.refs_1_, bf16[3200,768]{1,0:T(8,128)(2,1)S(1)} %get-tuple-element.49.refs_2_, bf16[3200,768]{1,0:T(8,128)(2,1)S(1)} %copy-done.1, ...), custom_call_target="tpu_custom_call" | custom-call | flops 1 | bytes 1 | tf_op jit(solution)/shard_map/far/pallas_call | solution.py:213
  70.5 0.9 %collective-permute-done.12.refs_1_ = f32[400,128]{1,0:T(8,128)S(1)} collective-permute-done((f32[400,128]{1,0:T(8,128)S(1)}, f32[400,128]{1,0:T(8,128)S(1)}, u32[]{:S(2)}, u32[]{:S(2)}) %collective-permute-start.12) | collective-permute-done | bytes 204832 | tf_op jit(solution)/shard_map/ppermute | solution.py:304
  71.3 5.1 %collective-permute-done.13.refs_2_ = f32[400,128]{1,0:T(8,128)S(1)} collective-permute-done((f32[400,128]{1,0:T(8,128)S(1)}, f32[400,128]{1,0:T(8,128)S(1)}, u32[]{:S(2)}, u32[]{:S(2)}) %collective-permute-start.13) | collective-permute-done | bytes 204832 | tf_op jit(solution)/shard_map/ppermute | solution.py:304
  76.4 0.2 collective-permute-done.14.refs_3_
  76.6 1.1 %finish.1 = (f32[1,800,128]{2,1,0:T(8,128)}, f32[1,800,128]{2,1,0:T(8,128)}) custom-call(f32[400,128]{1,0:T(8,128)S(1)} %add.1.near, f32[400,128]{1,0:T(8,128)S(1)} %far.5.refs_0_, f32[400,128]{1,0:T(8,128)S(1)} %collective-permute-done.12.refs_1_, f32[400,128]{1,0:T(8,128)S(1)} %collective-permute-done.13.refs_2_, ...), custom_call_target="tpu_custom_call" | custom-call | flops 1 | bytes 1 | tf_op jit(solution)/shard_map/finish/pallas_call | solution.py:291
  (22 shorter events, 0.4 us)
Async XLA Ops:
  0.6 1.4 %copy-start.2 = (f32[8,3200,16]{1,2,0:T(8,128)S(1)}, f32[8,3200,16]{1,2,0:T(8,128)}, u32[]{:S(2)}) copy-start(f32[8,3200,16]{1,2,0:T(8,128)} %param.6) | copy-start | bytes 4915204
  2.1 0.7 copy-start.3
  5.3 7.1 %collective-permute-start.1 = (f32[16,1536]{1,0:T(8,128)S(1)}, f32[16,1536]{1,0:T(8,128)S(1)}, u32[]{:S(2)}, u32[]{:S(2)}) collective-permute-start(f32[16,1536]{1,0:T(8,128)S(1)} %get-tuple-element.35), channel_id=1, source_target_pairs={{0,8},{4,12},{8,0},{12,4},{16,24},{20,28},{24,16},{28,20},{1,9},{5... | collective-permute-start | bytes 294920 | tf_op jit(solution)/shard_map/ppermute | solution.py:304
  8.4 4.9 %collective-permute-start.2 = (f32[16,1536]{1,0:T(8,128)S(1)}, f32[16,1536]{1,0:T(8,128)S(1)}, u32[]{:S(2)}, u32[]{:S(2)}) collective-permute-start(f32[16,1536]{1,0:T(8,128)S(1)} %get-tuple-element.36), channel_id=1, source_target_pairs={{0,12},{4,8},{8,4},{12,0},{16,28},{20,24},{24,20},{28,16},{1,13},{... | collective-permute-start | bytes 294920 | tf_op jit(solution)/shard_map/ppermute | solution.py:304
  8.4 15.2 %collective-permute-start = (f32[16,3200]{1,0:T(8,128)S(1)}, f32[16,3200]{1,0:T(8,128)S(1)}, u32[]{:S(2)}, u32[]{:S(2)}) collective-permute-start(f32[16,3200]{1,0:T(8,128)S(1)} %get-tuple-element.33), channel_id=1, source_target_pairs={{0,4},{4,0},{8,12},{12,8},{16,20},{20,16},{24,28},{28,24},{1,5},{5... | collective-permute-start | bytes 614408 | tf_op jit(solution)/shard_map/ppermute | solution.py:304
  10.0 0.7 copy-start.4
  13.3 5.4 %collective-permute-start.3 = (f32[16,1664]{1,0:T(8,128)S(1)}, f32[16,1664]{1,0:T(8,128)S(1)}, u32[]{:S(2)}, u32[]{:S(2)}) collective-permute-start(f32[16,1664]{1,0:T(8,128)S(1)} %get-tuple-element.37), channel_id=1, source_target_pairs={{0,8},{4,12},{8,0},{12,4},{16,24},{20,28},{24,16},{28,20},{1,9},{5... | collective-permute-start | bytes 319496 | tf_op jit(solution)/shard_map/ppermute | solution.py:304
  14.4 21.4 %collective-permute-start.4 = (f32[16,1664]{1,0:T(8,128)S(1)}, f32[16,1664]{1,0:T(8,128)S(1)}, u32[]{:S(2)}, u32[]{:S(2)}) collective-permute-start(f32[16,1664]{1,0:T(8,128)S(1)} %get-tuple-element.39), channel_id=1, source_target_pairs={{0,12},{4,8},{8,4},{12,0},{16,28},{20,24},{24,20},{28,16},{1,13},{... | collective-permute-start | bytes 319496 | tf_op jit(solution)/shard_map/ppermute | solution.py:304
  14.5 38.0 %collective-permute-start.8 = (f32[16,3200]{1,0:T(8,128)S(1)}, f32[16,3200]{1,0:T(8,128)S(1)}, u32[]{:S(2)}, u32[]{:S(2)}) collective-permute-start(f32[16,3200]{1,0:T(8,128)S(1)} %get-tuple-element.55), channel_id=1, source_target_pairs={{0,16},{4,20},{8,24},{12,28},{16,0},{20,4},{24,8},{28,12},{1,17},{... | collective-permute-start | bytes 614408 | tf_op jit(solution)/shard_map/ppermute | solution.py:304
  17.6 36.5 %collective-permute-start.9 = (f32[16,3200]{1,0:T(8,128)S(1)}, f32[16,3200]{1,0:T(8,128)S(1)}, u32[]{:S(2)}, u32[]{:S(2)}) collective-permute-start(f32[16,3200]{1,0:T(8,128)S(1)} %get-tuple-element.56), channel_id=1, source_target_pairs={{0,20},{4,16},{8,28},{12,24},{16,4},{20,0},{24,12},{28,8},{1,21},{... | collective-permute-start | bytes 614408 | tf_op jit(solution)/shard_map/ppermute | solution.py:304
  18.7 35.8 %collective-permute-start.10 = (f32[16,3200]{1,0:T(8,128)S(1)}, f32[16,3200]{1,0:T(8,128)S(1)}, u32[]{:S(2)}, u32[]{:S(2)}) collective-permute-start(f32[16,3200]{1,0:T(8,128)S(1)} %get-tuple-element.57), channel_id=1, source_target_pairs={{0,24},{4,28},{8,16},{12,20},{16,8},{20,12},{24,0},{28,4},{1,25},{... | collective-permute-start | bytes 614408 | tf_op jit(solution)/shard_map/ppermute | solution.py:304
  23.6 31.0 %collective-permute-start.11 = (f32[16,3200]{1,0:T(8,128)S(1)}, f32[16,3200]{1,0:T(8,128)S(1)}, u32[]{:S(2)}, u32[]{:S(2)}) collective-permute-start(f32[16,3200]{1,0:T(8,128)S(1)} %get-tuple-element.58), channel_id=1, source_target_pairs={{0,28},{4,24},{8,20},{12,16},{16,12},{20,8},{24,4},{28,0},{1,29},{... | collective-permute-start | bytes 614408 | tf_op jit(solution)/shard_map/ppermute | solution.py:304
  35.9 8.0 %copy-start = (bf16[3200,768]{1,0:T(8,128)(2,1)}, bf16[3200,768]{1,0:T(8,128)(2,1)S(1)}, u32[]{:S(2)}) copy-start(bf16[3200,768]{1,0:T(8,128)(2,1)S(1)} %get-tuple-element.50.refs_3_) | copy-start | bytes 14745604
  43.9 10.7 %copy-start.1 = (bf16[3200,768]{1,0:T(8,128)(2,1)S(1)}, bf16[3200,768]{1,0:T(8,128)(2,1)}, u32[]{:S(2)}) copy-start(bf16[3200,768]{1,0:T(8,128)(2,1)} %copy-done) | copy-start | bytes 14745604
  51.0 16.0 %collective-permute-start.5 = (f32[400,128]{1,0:T(8,128)S(1)}, f32[400,128]{1,0:T(8,128)S(1)}, u32[]{:S(2)}, u32[]{:S(2)}) collective-permute-start(f32[400,128]{1,0:T(8,128)S(1)} %get-tuple-element.44), channel_id=1, source_target_pairs={{0,1},{1,0},{2,3},{3,2},{4,5},{5,4},{6,7},{7,6},{8,9},{9,8},{10,11... | collective-permute-start | bytes 614408 | tf_op jit(solution)/shard_map/ppermute | solution.py:304
  52.6 14.9 %collective-permute-start.6 = (f32[400,128]{1,0:T(8,128)S(1)}, f32[400,128]{1,0:T(8,128)S(1)}, u32[]{:S(2)}, u32[]{:S(2)}) collective-permute-start(f32[400,128]{1,0:T(8,128)S(1)} %get-tuple-element.45), channel_id=1, source_target_pairs={{0,2},{1,3},{2,0},{3,1},{4,6},{5,7},{6,4},{7,5},{8,10},{9,11},{10,... | collective-permute-start | bytes 614408 | tf_op jit(solution)/shard_map/ppermute | solution.py:304
  54.1 13.3 %collective-permute-start.7 = (f32[400,128]{1,0:T(8,128)S(1)}, f32[400,128]{1,0:T(8,128)S(1)}, u32[]{:S(2)}, u32[]{:S(2)}) collective-permute-start(f32[400,128]{1,0:T(8,128)S(1)} %get-tuple-element.46), channel_id=1, source_target_pairs={{0,3},{1,2},{2,1},{3,0},{4,7},{5,6},{6,5},{7,4},{8,11},{9,10},{10,... | collective-permute-start | bytes 614408 | tf_op jit(solution)/shard_map/ppermute | solution.py:304
  63.9 7.4 %collective-permute-start.12 = (f32[400,128]{1,0:T(8,128)S(1)}, f32[400,128]{1,0:T(8,128)S(1)}, u32[]{:S(2)}, u32[]{:S(2)}) collective-permute-start(f32[400,128]{1,0:T(8,128)S(1)} %far.6), channel_id=1, source_target_pairs={{0,1},{1,0},{2,3},{3,2},{4,5},{5,4},{6,7},{7,6},{8,9},{9,8},{10,11... | collective-permute-start | bytes 614408 | tf_op jit(solution)/shard_map/ppermute | solution.py:304
  65.5 11.0 %collective-permute-start.13 = (f32[400,128]{1,0:T(8,128)S(1)}, f32[400,128]{1,0:T(8,128)S(1)}, u32[]{:S(2)}, u32[]{:S(2)}) collective-permute-start(f32[400,128]{1,0:T(8,128)S(1)} %far.7), channel_id=1, source_target_pairs={{0,2},{1,3},{2,0},{3,1},{4,6},{5,7},{6,4},{7,5},{8,10},{9,11},{10,... | collective-permute-start | bytes 614408 | tf_op jit(solution)/shard_map/ppermute | solution.py:304
  67.0 9.7 %collective-permute-start.14 = (f32[400,128]{1,0:T(8,128)S(1)}, f32[400,128]{1,0:T(8,128)S(1)}, u32[]{:S(2)}, u32[]{:S(2)}) collective-permute-start(f32[400,128]{1,0:T(8,128)S(1)} %get-tuple-element.61), channel_id=1, source_target_pairs={{0,3},{1,2},{2,1},{3,0},{4,7},{5,6},{6,5},{7,4},{8,11},{9,10},{10,... | collective-permute-start | bytes 614408 | tf_op jit(solution)/shard_map/ppermute | solution.py:304

commit v2 on v1

v2 whole, which is shorter than its diff:
```python
import functools

import jax
import jax.numpy as jnp
from jax import lax
from jax.experimental import pallas as pl
from jax.experimental.pallas import tpu as pltpu
from jax.sharding import PartitionSpec as P

NIRR = 8
VI = 40
OI = 4
F32 = jnp.float32
BF16 = jnp.bfloat16
ANY = pl.BlockSpec(memory_space=pl.ANY)
PREP_MIB = 56
NEAR_MIB = 14
STEP = 768
COLUMNS_MIB = 5
FAR_MIB = 4
LAST_MIB = 32
SMALL_MIB = 4
SMEM = pl.BlockSpec(memory_space=pltpu.SMEM)
VMEM = pl.BlockSpec(memory_space=pltpu.VMEM)
FAR = (4, 5, 6, 7)
RING = 3


def cost(flops, nbytes):
    return pl.CostEstimate(flops=1, bytes_accessed=1, transcendentals=0)


def params(mib):
    return pltpu.CompilerParams(vmem_limit_bytes=mib * 1024 * 1024)


def denominator(block, groups, ab_block, start, count, columns, vir_energy, occ_energy):
    irrep = block // groups
    rows = block % groups * ab_block + start + jnp.arange(count, dtype=jnp.int32)
    arow = rows // (VI * VI)
    first = arow * VI + rows // VI % VI
    second = jnp.bitwise_xor(arow, irrep) * VI + rows % VI
    cols = jnp.arange(columns, dtype=jnp.int32)
    orow = cols // (OI * OI)
    hole_one = orow * OI + cols // OI % OI
    hole_two = jnp.bitwise_xor(orow, irrep) * OI + cols % OI
    upper = jnp.take(vir_energy, first) + jnp.take(vir_energy, second)
    lower = jnp.take(occ_energy, hole_one) + jnp.take(occ_energy, hole_two)
    return upper[:, None] - lower[None, :]


def general(integrals, amplitudes, blockmap, vir_energy, occ_energy):
    blocks = lax.axis_size("blk")
    groups = blocks // NIRR
    block = blockmap[lax.axis_index("blk")]
    local = integrals[0]
    ab_block = local.shape[0]
    share = ab_block // lax.axis_size("ctr")
    wanted = jnp.take(amplitudes, blockmap // groups, axis=0)
    parts = lax.all_to_all(wanted, "blk", 0, 0)
    chosen = jnp.moveaxis(parts, 0, 1).reshape(parts.shape[1], -1)
    partial_value = jnp.dot(local, chosen, preferred_element_type=F32, precision=lax.Precision.HIGHEST)
    mine = lax.psum_scatter(partial_value, "ctr", scatter_dimension=0, tiled=True)
    offset = lax.axis_index("ctr") * share
    denom = denominator(block, groups, ab_block, offset, share, mine.shape[1], vir_energy, occ_energy)
    return (mine[None], (mine / denom)[None])


def prep_kernel(bm, amps, *refs):
    near, far, sem = refs[0], refs[1:5], refs[5]
    me = lax.axis_index("blk")
    copies = [(amps.at[bm[jnp.bitwise_or(jnp.bitwise_and(me, 4), m)]], near.at[m]) for m in range(4)]
    copies += [(amps.at[bm[jnp.bitwise_xor(me, s)]], out) for s, out in zip(FAR, far)]
    copies = [pltpu.make_async_copy(x, y, sem.at[n]) for n, (x, y) in enumerate(copies)]
    for c in copies:
        c.start()
    for c in copies:
        c.wait()


def prep(blockmap, amps):
    one = amps.shape[1:]
    out = pl.pallas_call(
        prep_kernel,
        out_shape=[jax.ShapeDtypeStruct((4, *one), F32)] + [jax.ShapeDtypeStruct(one, F32)] * 4,
        in_specs=[SMEM, ANY],
        out_specs=[VMEM] * 5,
        scratch_shapes=[pltpu.SemaphoreType.DMA((8,))],
        compiler_params=params(PREP_MIB),
        cost_estimate=cost(0, 2 * 4 * amps.size),
        name="prep",
    )(blockmap, amps)
    return out[0], out[1:]


def split(x):
    hi = x.astype(BF16)
    return hi, (x - hi.astype(F32)).astype(BF16)


def columns(sources):
    hi, lo = split(jnp.concatenate(sources, 0).T)
    return jnp.concatenate([hi, lo], 1)


def columns_kernel(*refs):
    pieces, w = refs[:4], refs[4]
    source = [jnp.bitwise_and(jnp.bitwise_xor(lax.axis_index("blk"), s), 3) for s in FAR]
    sources = []
    for q in range(4):
        x = pieces[3][...]
        for n in range(3):
            x = jnp.where(source[n] == q, pieces[n][...], x)
        sources.append(x)
    w[...] = columns(sources)


def columns_of(pieces):
    return pl.pallas_call(
        columns_kernel,
        out_shape=jax.ShapeDtypeStruct((pieces[0].shape[1], 128), BF16),
        in_specs=[VMEM] * 4,
        out_specs=VMEM,
        compiler_params=params(COLUMNS_MIB),
        cost_estimate=cost(0, 0),
        name="columns",
    )(*pieces)


def fold(wide):
    value = wide + pltpu.roll(wide, 64, 1)
    half = value.shape[0] // 2
    left = lax.broadcasted_iota(jnp.int32, (half, 128), 1) < 64
    return jnp.where(left, value[:half], value[half:])


def near_kernel(spans, a, piece, his, los, *refs):
    outs, (buf, w, last, acc, sem) = refs[:4], refs[4:]
    ctr = lax.axis_index("ctr")
    share = a.shape[0] // 4

    def load(n, s):
        k0, kc = spans[n]
        at = lax.rem(4 * n + s, RING)
        row = pl.multiple_of(jnp.bitwise_xor(ctr, 3 - s) * share, share)
        return pltpu.make_async_copy(
            a.at[pl.ds(row, share), pl.ds(k0, kc)], buf.at[at, :, pl.ds(0, kc)], sem.at[at]
        )

    for s in range(RING):
        load(0, s).start()
    for k0, kc in spans:
        w[k0 : k0 + kc, :] = columns([piece[m, :, k0 : k0 + kc] for m in range(4)])
    for n, (k0, kc) in enumerate(spans):
        cols = slice(k0, k0 + kc)

        def step(s, keep_hi, keep_lo, at, wide_cols):
            load(n, s).wait()
            hi, lo = split(buf[lax.rem(4 * n + s, RING), :, :kc])
            keep_hi[at, wide_cols] = hi
            keep_lo[at, wide_cols] = lo

            @pl.when(s + RING < 4)
            def _():
                load(n, s + RING).start()

            if n + 1 < len(spans):

                @pl.when(s + RING >= 4)
                def _():
                    load(n + 1, s + RING - 4).start()

            wide = jnp.dot(keep_hi[at, wide_cols], w[cols, :], preferred_element_type=F32)
            return fold(wide + jnp.dot(keep_lo[at, wide_cols], w[cols, :], preferred_element_type=F32))

        @pl.loop(0, 3)
        def _(s):
            x = step(s, his, los, pl.ds(pl.multiple_of(s * share, share), share), cols)
            acc[s] = acc[s] + x if n else x

        x = step(3, last.at[0], last.at[1], slice(None), slice(0, kc))
        outs[0][...] = outs[0][...] + x if n else x

    for s in range(3):
        outs[3 - s][...] = acc[s]

def near_pass(a, piece):
    rows, cd = a.shape
    spans = [(k0, min(STEP, cd - k0)) for k0 in range(0, cd, STEP)]
    kept = jax.ShapeDtypeStruct((rows // 4 * 3, cd), BF16)
    packed = (rows // 8, 128)
    widest = max(kc for _, kc in spans)
    out = pl.pallas_call(
        functools.partial(near_kernel, spans),
        out_shape=[kept, kept] + [jax.ShapeDtypeStruct(packed, F32)] * 4,
        in_specs=[ANY, VMEM],
        out_specs=[VMEM] * 6,
        scratch_shapes=[
            pltpu.VMEM((RING, rows // 4, widest), F32),
            pltpu.VMEM((cd, 128), BF16),
            pltpu.VMEM((2, rows // 4, widest), BF16),
            pltpu.VMEM((3, *packed), F32),
            pltpu.SemaphoreType.DMA((RING,)),
        ],
        compiler_params=params(NEAR_MIB),
        cost_estimate=cost(0, 0),
        name="near",
    )(a, piece)
    return out[:2], out[2:]


def far_kernel(s, hi, lo, w, out):
    share = out.shape[0] * 2
    at = slice((3 - s) * share, (4 - s) * share)
    wide = jnp.dot(hi[at, :], w[...], preferred_element_type=F32)
    out[...] = fold(wide + jnp.dot(lo[at, :], w[...], preferred_element_type=F32))


def far_tile(kept, s, w):
    rows = kept[0].shape[0]
    return pl.pallas_call(
        functools.partial(far_kernel, s),
        out_shape=jax.ShapeDtypeStruct((rows // 6, 128), F32),
        in_specs=[VMEM] * 3,
        out_specs=VMEM,
        compiler_params=params(FAR_MIB),
        cost_estimate=cost(0, 0),
        name="far",
    )(*kept, w)


def last_kernel(spans, a, w, out, buf, wide, sem):
    share = buf.shape[0]
    row = pl.multiple_of(lax.axis_index("ctr") * share, share)
    loads = [
        pltpu.make_async_copy(a.at[pl.ds(row, share), pl.ds(*span)], buf.at[:, pl.ds(*span)], sem.at[n])
        for n, span in enumerate(spans)
    ]
    for x in loads:
        x.start()
    for n, (x, (k0, kc)) in enumerate(zip(loads, spans)):
        x.wait()
        hi, lo = split(buf[:, k0 : k0 + kc])
        part = jnp.dot(hi, w[k0 : k0 + kc, :], preferred_element_type=F32)
        part = part + jnp.dot(lo, w[k0 : k0 + kc, :], preferred_element_type=F32)
        wide[...] = wide[...] + part if n else part
    out[...] = fold(wide[...])


def last_tile(a, w):
    rows, cd = a.shape
    spans = ranges(cd, 6)
    return pl.pallas_call(
        functools.partial(last_kernel, spans),
        out_shape=jax.ShapeDtypeStruct((rows // 8, 128), F32),
        in_specs=[ANY, VMEM],
        out_specs=VMEM,
        scratch_shapes=[
            pltpu.VMEM((rows // 4, cd), F32),
            pltpu.VMEM((rows // 4, 128), F32),
            pltpu.SemaphoreType.DMA((len(spans),)),
        ],
        compiler_params=params(LAST_MIB),
        cost_estimate=cost(0, 0),
        name="last",
    )(a, w)


def denom_kernel(count, bm, vir, occ, out):
    irrep = bm[lax.axis_index("blk")]
    start = lax.axis_index("ctr") * count
    vir_at = lax.broadcasted_iota(jnp.int32, (count, vir.shape[1]), 1)
    rows = start + lax.broadcasted_iota(jnp.int32, (count, vir.shape[1]), 0)
    arow = rows // (VI * VI)
    first = arow * VI + rows // VI % VI
    second = jnp.bitwise_xor(arow, irrep) * VI + rows % VI
    energy = jnp.broadcast_to(vir[...], vir_at.shape)
    pick = lambda at: jnp.sum(jnp.where(vir_at == at, energy, 0.0), axis=1, keepdims=True)
    upper = pick(first) + pick(second)
    occ_at = lax.broadcasted_iota(jnp.int32, (occ.shape[0], 128), 0)
    cols = lax.broadcasted_iota(jnp.int32, (occ.shape[0], 128), 1)
    orow = cols // (OI * OI)
    hole_one = orow * OI + cols // OI % OI
    hole_two = jnp.bitwise_xor(orow, irrep) * OI + cols % OI
    level = jnp.broadcast_to(occ[...], occ_at.shape)
    find = lambda at: jnp.sum(jnp.where(occ_at == at, level, 0.0), axis=0, keepdims=True)
    lower = find(hole_one) + find(hole_two)
    out[...] = upper - lower


def denominators(blockmap, vir_energy, occ_energy, count):
    return pl.pallas_call(
        functools.partial(denom_kernel, count),
        out_shape=jax.ShapeDtypeStruct((count, 128), F32),
        in_specs=[SMEM, VMEM, VMEM],
        out_specs=VMEM,
        compiler_params=params(8),
        cost_estimate=cost(count * 320 * 8, count * 128 * 4),
        name="denominators",
    )(blockmap, vir_energy.reshape(1, -1), occ_energy.reshape(-1, 1))


def add_kernel(*refs):
    refs[4][...] = (refs[0][...] + refs[1][...]) + (refs[2][...] + refs[3][...])


def add(parts):
    x = parts[0]
    return pl.pallas_call(
        add_kernel,
        out_shape=jax.ShapeDtypeStruct(x.shape, F32),
        in_specs=[VMEM] * 4,
        out_specs=VMEM,
        compiler_params=params(SMALL_MIB),
        cost_estimate=cost(4 * x.size, 20 * x.size),
        name="add",
    )(*parts)


def finish_kernel(near, *refs):
    far, denom, ladder, inc = refs[:4], *refs[4:]
    low = lax.axis_index("blk") // 4 == 0
    near = near[...]
    far = (far[0][...] + far[1][...]) + (far[2][...] + far[3][...])
    one, two = jnp.where(low, near, far), jnp.where(low, far, near)
    rows = near.shape[0]
    left = lax.broadcasted_iota(jnp.int32, (rows, 128), 1) < 64
    values = (jnp.where(left, one, pltpu.roll(two, 64, 1)), jnp.where(left, pltpu.roll(one, 64, 1), two))
    for n, value in enumerate(values):
        at = slice(n * rows, (n + 1) * rows)
        ladder[0, at] = value
        inc[0, at] = value / denom[at]


def finish(near, far, denom):
    out = jax.ShapeDtypeStruct((1, *denom.shape), F32)
    return pl.pallas_call(
        finish_kernel,
        out_shape=[out, out],
        in_specs=[VMEM] * 6,
        out_specs=[VMEM] * 2,
        compiler_params=params(8),
        cost_estimate=cost(denom.size * 8, denom.size * 4 * 7),
        name="finish",
    )(near, *far, denom)


def swap(x, axis, s):
    n = lax.axis_size(axis)
    return lax.ppermute(x, axis, [(i, i ^ s) for i in range(n)])


def after(x, *first):
    return lax.optimization_barrier((x, *first))[0]


def ranges(total, parts):
    tiles = total // 128
    edges = [n * tiles // parts * 128 for n in range(parts + 1)]
    return [(a, b - a) for a, b in zip(edges, edges[1:])]


def special(integrals, amplitudes, blockmap, vir_energy, occ_energy):
    a = integrals[0]
    amps = jnp.swapaxes(amplitudes, 1, 2)
    to_near, to_far = prep(blockmap, amps)
    near = lax.all_to_all(to_near, "blk", 0, 0, axis_index_groups=[[0, 1, 2, 3], [4, 5, 6, 7]])
    denom = denominators(blockmap, vir_energy, occ_energy, a.shape[0] // 4)
    far = [swap(after(x, denom), "blk", s) for s, x in zip(FAR, to_far)]
    kept, sums = near_pass(a, near)
    near_sum = add([sums[0], *[swap(sums[s], "ctr", s) for s in (1, 2, 3)]])
    w = columns_of(far)
    far_sums = {}
    for s in (3, 1, 2):
        mine = far_tile(kept, s, w)
        far_sums[s] = swap(mine, "ctr", s)
    far_sums[0] = last_tile(a, after(w, near_sum, far_sums[3], mine))
    return tuple(finish(near_sum, [far_sums[s] for s in range(4)], denom))


def on_device(integrals, amplitudes, *rest):
    _, rows, cd = integrals.shape
    fits = (
        lax.axis_size("blk") == NIRR
        and lax.axis_size("ctr") == 4
        and rows % 128 == 0
        and cd % 128 == 0
        and amplitudes.shape[2] == 16
    )
    return (special if fits else general)(integrals, amplitudes, *rest)


def solution(mesh):
    placed = (P("blk", None, "ctr"), P(None, "ctr", "blk"), P(), P(), P())
    return jax.shard_map(
        on_device,
        mesh=mesh,
        in_specs=placed,
        out_specs=(P("blk", "ctr", None), P("blk", "ctr", None)),
        check_vma=False,
    )
```

time: 78.6 us -> 76.7 us (0.976)
  the two profiles are of different devices: /device:TPU:0 before, /device:TPU:22 now
where the time goes in v2:
time: 76.7 us; the launch traced here: 76.4 us
  Pallas kernels  41.5 us (54%)
  waiting for transfers between devices  18 us (23%)
  starting transfers between devices  14.2 us (19%)
  local copies, waits for them, and re-layouts  2.08 us (3%)
    pallas_call x1, Pallas kernels, near_pass(): pl.pallas_call(functools.partial(near_kernel, spans), out_shape=[kept, ke...  18.1 us
    ppermute x10, waiting for transfers between devices, swap(): return lax.ppermute(x, axis, [(i, i ^ s) for i in range(n)])  13.8 us
    ppermute x10, starting transfers between devices, swap(): return lax.ppermute(x, axis, [(i, i ^ s) for i in range(n)])  10.7 us
    pallas_call x3, Pallas kernels, far_tile(): pl.pallas_call(functools.partial(far_kernel, s), out_shape=jax.ShapeDtype...  8.68 us
    pallas_call x1, Pallas kernels, last_tile(): pl.pallas_call(functools.partial(last_kernel, spans), out_shape=jax.Shape...  7.67 us
    all_to_all x1, waiting for transfers between devices, special(): lax.all_to_all(to_near, 'blk', 0, 0, axis_index_groups=[[0, 1, 2, 3], [4,...  4.19 us
    all_to_all x1, starting transfers between devices, special(): lax.all_to_all(to_near, 'blk', 0, 0, axis_index_groups=[[0, 1, 2, 3], [4,...  3.51 us
    pallas_call x1, Pallas kernels, prep(): pl.pallas_call(prep_kernel, out_shape=[jax.ShapeDtypeStruct((4, *one), F3...  3.39 us
  transfers between devices with their start and end apart: 11, of which 5 were waited for; matrix products, arithmetic and copies ran while one was open for 2% of the time, Pallas kernels for 48%

profile of v2, /device:TPU:22, one launch (start us, length us, event | category | flops | bytes accessed | tf_op | source)
XLA Modules:
  0.0 76.4 jit_solution(10768573163962343094)
XLA Ops:
  0.6 3.4 %prep.1 = (f32[4,16,3200]{2,1,0:T(8,128)}, f32[16,3200]{1,0:T(8,128)}, f32[16,3200]{1,0:T(8,128)}, f32[16,3200]{1,0:T(8,128)}, f32[16,3200]{1,0:T(8,128)}) custom-call(s32[8]{0:T(128)} %bm.3, f32[8,16,3200]{2,1,0:T(8,128)} %bitcast.5), custom_call_target="tpu_custom_call" | custom-call | flops 1 | bytes 1 | tf_op jit(solution)/shard_map/prep/pallas_call | solution.py:83
  4.0 3.5 %all-to-all-start = ((f32[4,16,3200]{2,1,0:T(8,128)}), f32[4,16,3200]{2,1,0:T(8,128)S(1)}, u32[]{:S(2)}, u32[]{:S(2)}) async-start(f32[4,16,3200]{2,1,0:T(8,128)} %get-tuple-element.18), calls=%async_computation | async-start | bytes 1638400 | tf_op jit(solution)/shard_map/all_to_all | solution.py:367
  7.5 0.7 reshape.10.vir
  8.2 0.7 copy.7.occ
  9.0 0.7 copy-done
  9.6 1.7 %denominators.1.refs_4_ = f32[800,128]{1,0:T(8,128)S(1)} custom-call(s32[8]{0:T(128)S(1)} %copy-done, f32[1,320]{1,0:T(1,128)S(1)} %reshape.10.vir, f32[32,1]{1,0:T(8,128)S(1)} %copy.7.occ), custom_call_target="tpu_custom_call" | custom-call | flops 1 | bytes 1 | tf_op jit(solution)/shard_map/denominators/pallas_call | solution.py:292
  11.3 0.4 collective-permute-start.3
  11.7 2.4 %collective-permute-start.4 = (f32[16,3200]{1,0:T(8,128)}, f32[16,3200]{1,0:T(8,128)S(1)}, u32[]{:S(2)}, u32[]{:S(2)}) collective-permute-start(f32[16,3200]{1,0:T(8,128)} %get-tuple-element.26), channel_id=1, source_target_pairs={{0,20},{4,16},{8,28},{12,24},{16,4},{20,0},{24,12},{28,8},{1,21},{... | collective-permute-start | bytes 614408 | tf_op jit(solution)/shard_map/ppermute | solution.py:350
  14.1 0.7 collective-permute-start.5
  14.9 0.9 %collective-permute-start.6 = (f32[16,3200]{1,0:T(8,128)}, f32[16,3200]{1,0:T(8,128)S(1)}, u32[]{:S(2)}, u32[]{:S(2)}) collective-permute-start(f32[16,3200]{1,0:T(8,128)} %get-tuple-element.30), channel_id=1, source_target_pairs={{0,28},{4,24},{8,20},{12,16},{16,12},{20,8},{24,4},{28,0},{1,29},{... | collective-permute-start | bytes 614408 | tf_op jit(solution)/shard_map/ppermute | solution.py:350
  15.8 4.2 %all-to-all-done.piece = f32[4,16,3200]{2,1,0:T(8,128)S(1)} async-done(((f32[4,16,3200]{2,1,0:T(8,128)}), f32[4,16,3200]{2,1,0:T(8,128)S(1)}, u32[]{:S(2)}, u32[]{:S(2)}) %all-to-all-start) | async-done | bytes 819232 | tf_op jit(solution)/shard_map/all_to_all | solution.py:367
  20.0 18.1 %near.1 = (bf16[2400,3200]{1,0:T(8,128)(2,1)S(1)}, bf16[2400,3200]{1,0:T(8,128)(2,1)S(1)}, f32[400,128]{1,0:T(8,128)S(1)}, f32[400,128]{1,0:T(8,128)S(1)}, f32[4...) custom-call(f32[3200,3200]{1,0:T(8,128)} %bitcast.3, f32[4,16,3200]{2,1,0:T(8,128)S(1)} %all-to-all-done.piece), custom_call_target="tpu_custom_call" | custom-call | flops 1 | bytes 1 | tf_op jit(solution)/shard_map/near/pallas_call | solution.py:193
  38.1 0.5 collective-permute-start
  38.7 0.0 collective-permute-done.3.refs_0_
  38.7 0.8 collective-permute-done.4.refs_1_
  39.4 7.9 %collective-permute-done.5.refs_2_ = f32[16,3200]{1,0:T(8,128)S(1)} collective-permute-done((f32[16,3200]{1,0:T(8,128)}, f32[16,3200]{1,0:T(8,128)S(1)}, u32[]{:S(2)}, u32[]{:S(2)}) %collective-permute-start.5) | collective-permute-done | bytes 204832 | tf_op jit(solution)/shard_map/ppermute | solution.py:350
  47.3 2.8 %collective-permute-done.6.refs_3_ = f32[16,3200]{1,0:T(8,128)S(1)} collective-permute-done((f32[16,3200]{1,0:T(8,128)}, f32[16,3200]{1,0:T(8,128)S(1)}, u32[]{:S(2)}, u32[]{:S(2)}) %collective-permute-start.6) | collective-permute-done | bytes 204832 | tf_op jit(solution)/shard_map/ppermute | solution.py:350
  50.1 0.7 columns.1.w
  50.9 0.6 collective-permute-start.1
  51.4 1.5 %collective-permute-start.2 = (f32[400,128]{1,0:T(8,128)S(1)}, f32[400,128]{1,0:T(8,128)S(1)}, u32[]{:S(2)}, u32[]{:S(2)}) collective-permute-start(f32[400,128]{1,0:T(8,128)S(1)} %get-tuple-element.22), channel_id=1, source_target_pairs={{0,3},{1,2},{2,1},{3,0},{4,7},{5,6},{6,5},{7,4},{8,11},{9,10},{10,... | collective-permute-start | bytes 614408 | tf_op jit(solution)/shard_map/ppermute | solution.py:350
  52.9 2.9 %far.3 = f32[400,128]{1,0:T(8,128)S(1)} custom-call(bf16[2400,3200]{1,0:T(8,128)(2,1)S(1)} %get-tuple-element.31.hi, bf16[2400,3200]{1,0:T(8,128)(2,1)S(1)} %get-tuple-element.32.lo, bf16[3200,128]{1,0:T(8,128)(2,1)S(1)} %columns.1.w), custom_call_target="tpu_custom_call" | custom-call | flops 1 | bytes 1 | tf_op jit(solution)/shard_map/far/pallas_call | solution.py:221
  55.8 1.5 %collective-permute-start.7 = (f32[400,128]{1,0:T(8,128)S(1)}, f32[400,128]{1,0:T(8,128)S(1)}, u32[]{:S(2)}, u32[]{:S(2)}) collective-permute-start(f32[400,128]{1,0:T(8,128)S(1)} %far.3), channel_id=1, source_target_pairs={{0,3},{1,2},{2,1},{3,0},{4,7},{5,6},{6,5},{7,4},{8,11},{9,10},{10,... | collective-permute-start | bytes 614408 | tf_op jit(solution)/shard_map/ppermute | solution.py:350
  57.3 2.9 %far.4 = f32[400,128]{1,0:T(8,128)S(1)} custom-call(bf16[2400,3200]{1,0:T(8,128)(2,1)S(1)} %get-tuple-element.31.hi, bf16[2400,3200]{1,0:T(8,128)(2,1)S(1)} %get-tuple-element.32.lo, bf16[3200,128]{1,0:T(8,128)(2,1)S(1)} %columns.1.w), custom_call_target="tpu_custom_call" | custom-call | flops 1 | bytes 1 | tf_op jit(solution)/shard_map/far/pallas_call | solution.py:221
  60.2 2.9 %far.5 = f32[400,128]{1,0:T(8,128)S(1)} custom-call(bf16[2400,3200]{1,0:T(8,128)(2,1)S(1)} %get-tuple-element.31.hi, bf16[2400,3200]{1,0:T(8,128)(2,1)S(1)} %get-tuple-element.32.lo, bf16[3200,128]{1,0:T(8,128)(2,1)S(1)} %columns.1.w), custom_call_target="tpu_custom_call" | custom-call | flops 1 | bytes 1 | tf_op jit(solution)/shard_map/far/pallas_call | solution.py:221
  63.1 0.6 collective-permute-start.8
  63.7 0.0 collective-permute-done.refs_1_
  63.7 1.5 %collective-permute-start.9 = (f32[400,128]{1,0:T(8,128)S(1)}, f32[400,128]{1,0:T(8,128)S(1)}, u32[]{:S(2)}, u32[]{:S(2)}) collective-permute-start(f32[400,128]{1,0:T(8,128)S(1)} %far.4), channel_id=1, source_target_pairs={{0,2},{1,3},{2,0},{3,1},{4,6},{5,7},{6,4},{7,5},{8,10},{9,11},{10,... | collective-permute-start | bytes 614408 | tf_op jit(solution)/shard_map/ppermute | solution.py:350
  65.3 2.3 %collective-permute-done.1.refs_2_ = f32[400,128]{1,0:T(8,128)S(1)} collective-permute-done((f32[400,128]{1,0:T(8,128)S(1)}, f32[400,128]{1,0:T(8,128)S(1)}, u32[]{:S(2)}, u32[]{:S(2)}) %collective-permute-start.1) | collective-permute-done | bytes 204832 | tf_op jit(solution)/shard_map/ppermute | solution.py:350
  67.6 0.0 collective-permute-done.2.refs_3_
  67.6 7.7 %last.1.refs_0_ = f32[400,128]{1,0:T(8,128)S(1)} custom-call(f32[3200,3200]{1,0:T(8,128)} %bitcast.4, bf16[3200,128]{1,0:T(8,128)(2,1)S(1)} %columns.1.w), custom_call_target="tpu_custom_call" | custom-call | flops 1 | bytes 1 | tf_op jit(solution)/shard_map/last/pallas_call | solution.py:253
  75.3 0.0 collective-permute-done.8.refs_1_
  75.3 1.1 %finish.1 = (f32[1,800,128]{2,1,0:T(8,128)}, f32[1,800,128]{2,1,0:T(8,128)}) custom-call(f32[400,128]{1,0:T(8,128)S(1)} %add.1.near, f32[400,128]{1,0:T(8,128)S(1)} %last.1.refs_0_, f32[400,128]{1,0:T(8,128)S(1)} %collective-permute-done.8.refs_1_, f32[400,128]{1,0:T(8,128)S(1)} %collective-permute-done.9.refs_2_, ...), custom_call_target="tpu_custom_call" | custom-call | flops 1 | bytes 1 | tf_op jit(solution)/shard_map/finish/pallas_call | solution.py:337
  (4 shorter events, 0.1 us)
Async XLA Ops:
  4.0 16.0 %all-to-all-start = ((f32[4,16,3200]{2,1,0:T(8,128)}), f32[4,16,3200]{2,1,0:T(8,128)S(1)}, u32[]{:S(2)}, u32[]{:S(2)}) async-start(f32[4,16,3200]{2,1,0:T(8,128)} %get-tuple-element.18), calls=%async_computation | async-start | bytes 1638400 | tf_op jit(solution)/shard_map/all_to_all | solution.py:367
  9.0 0.7 copy-start
  11.3 27.3 %collective-permute-start.3 = (f32[16,3200]{1,0:T(8,128)}, f32[16,3200]{1,0:T(8,128)S(1)}, u32[]{:S(2)}, u32[]{:S(2)}) collective-permute-start(f32[16,3200]{1,0:T(8,128)} %get-tuple-element.24), channel_id=1, source_target_pairs={{0,16},{4,20},{8,24},{12,28},{16,0},{20,4},{24,8},{28,12},{1,17},{... | collective-permute-start | bytes 614408 | tf_op jit(solution)/shard_map/ppermute | solution.py:350
  11.7 27.7 %collective-permute-start.4 = (f32[16,3200]{1,0:T(8,128)}, f32[16,3200]{1,0:T(8,128)S(1)}, u32[]{:S(2)}, u32[]{:S(2)}) collective-permute-start(f32[16,3200]{1,0:T(8,128)} %get-tuple-element.26), channel_id=1, source_target_pairs={{0,20},{4,16},{8,28},{12,24},{16,4},{20,0},{24,12},{28,8},{1,21},{... | collective-permute-start | bytes 614408 | tf_op jit(solution)/shard_map/ppermute | solution.py:350
  14.1 33.2 %collective-permute-start.5 = (f32[16,3200]{1,0:T(8,128)}, f32[16,3200]{1,0:T(8,128)S(1)}, u32[]{:S(2)}, u32[]{:S(2)}) collective-permute-start(f32[16,3200]{1,0:T(8,128)} %get-tuple-element.28), channel_id=1, source_target_pairs={{0,24},{4,28},{8,16},{12,20},{16,8},{20,12},{24,0},{28,4},{1,25},{... | collective-permute-start | bytes 614408 | tf_op jit(solution)/shard_map/ppermute | solution.py:350
  14.9 35.3 %collective-permute-start.6 = (f32[16,3200]{1,0:T(8,128)}, f32[16,3200]{1,0:T(8,128)S(1)}, u32[]{:S(2)}, u32[]{:S(2)}) collective-permute-start(f32[16,3200]{1,0:T(8,128)} %get-tuple-element.30), channel_id=1, source_target_pairs={{0,28},{4,24},{8,20},{12,16},{16,12},{20,8},{24,4},{28,0},{1,29},{... | collective-permute-start | bytes 614408 | tf_op jit(solution)/shard_map/ppermute | solution.py:350
  38.1 25.6 %collective-permute-start = (f32[400,128]{1,0:T(8,128)S(1)}, f32[400,128]{1,0:T(8,128)S(1)}, u32[]{:S(2)}, u32[]{:S(2)}) collective-permute-start(f32[400,128]{1,0:T(8,128)S(1)} %get-tuple-element.20), channel_id=1, source_target_pairs={{0,1},{1,0},{2,3},{3,2},{4,5},{5,4},{6,7},{7,6},{8,9},{9,8},{10,11... | collective-permute-start | bytes 614408 | tf_op jit(solution)/shard_map/ppermute | solution.py:350
  50.9 16.7 %collective-permute-start.1 = (f32[400,128]{1,0:T(8,128)S(1)}, f32[400,128]{1,0:T(8,128)S(1)}, u32[]{:S(2)}, u32[]{:S(2)}) collective-permute-start(f32[400,128]{1,0:T(8,128)S(1)} %get-tuple-element.21), channel_id=1, source_target_pairs={{0,2},{1,3},{2,0},{3,1},{4,6},{5,7},{6,4},{7,5},{8,10},{9,11},{10,... | collective-permute-start | bytes 614408 | tf_op jit(solution)/shard_map/ppermute | solution.py:350
  51.4 16.1 %collective-permute-start.2 = (f32[400,128]{1,0:T(8,128)S(1)}, f32[400,128]{1,0:T(8,128)S(1)}, u32[]{:S(2)}, u32[]{:S(2)}) collective-permute-start(f32[400,128]{1,0:T(8,128)S(1)} %get-tuple-element.22), channel_id=1, source_target_pairs={{0,3},{1,2},{2,1},{3,0},{4,7},{5,6},{6,5},{7,4},{8,11},{9,10},{10,... | collective-permute-start | bytes 614408 | tf_op jit(solution)/shard_map/ppermute | solution.py:350
  55.8 11.8 %collective-permute-start.7 = (f32[400,128]{1,0:T(8,128)S(1)}, f32[400,128]{1,0:T(8,128)S(1)}, u32[]{:S(2)}, u32[]{:S(2)}) collective-permute-start(f32[400,128]{1,0:T(8,128)S(1)} %far.3), channel_id=1, source_target_pairs={{0,3},{1,2},{2,1},{3,0},{4,7},{5,6},{6,5},{7,4},{8,11},{9,10},{10,... | collective-permute-start | bytes 614408 | tf_op jit(solution)/shard_map/ppermute | solution.py:350
  63.1 12.2 %collective-permute-start.8 = (f32[400,128]{1,0:T(8,128)S(1)}, f32[400,128]{1,0:T(8,128)S(1)}, u32[]{:S(2)}, u32[]{:S(2)}) collective-permute-start(f32[400,128]{1,0:T(8,128)S(1)} %far.5), channel_id=1, source_target_pairs={{0,1},{1,0},{2,3},{3,2},{4,5},{5,4},{6,7},{7,6},{8,9},{9,8},{10,11... | collective-permute-start | bytes 614408 | tf_op jit(solution)/shard_map/ppermute | solution.py:350
  63.7 11.6 %collective-permute-start.9 = (f32[400,128]{1,0:T(8,128)S(1)}, f32[400,128]{1,0:T(8,128)S(1)}, u32[]{:S(2)}, u32[]{:S(2)}) collective-permute-start(f32[400,128]{1,0:T(8,128)S(1)} %far.4), channel_id=1, source_target_pairs={{0,2},{1,3},{2,0},{3,1},{4,6},{5,7},{6,4},{7,5},{8,10},{9,11},{10,... | collective-permute-start | bytes 614408 | tf_op jit(solution)/shard_map/ppermute | solution.py:350

commit v3 on v2

--- a/solution.py
+++ b/solution.py
@@ -15,7 +15,6 @@
 ANY = pl.BlockSpec(memory_space=pl.ANY)
 PREP_MIB = 56
 NEAR_MIB = 14
-STEP = 768
 COLUMNS_MIB = 5
 FAR_MIB = 4
 LAST_MIB = 32
@@ -135,58 +134,54 @@
 
 
 def near_kernel(spans, a, piece, his, los, *refs):
-    outs, (buf, w, last, acc, sem) = refs[:4], refs[4:]
+    outs, (buf, w, acc, sem) = refs[:4], refs[4:]
     ctr = lax.axis_index("ctr")
     share = a.shape[0] // 4
 
-    def load(n, s):
+    def load(n, t):
         k0, kc = spans[n]
-        at = lax.rem(4 * n + s, RING)
-        row = pl.multiple_of(jnp.bitwise_xor(ctr, 3 - s) * share, share)
+        at = lax.rem(4 * n + t, RING)
+        row = pl.multiple_of(jnp.bitwise_xor(ctr, jnp.bitwise_and(4 - t, 3)) * share, share)
         return pltpu.make_async_copy(
             a.at[pl.ds(row, share), pl.ds(k0, kc)], buf.at[at, :, pl.ds(0, kc)], sem.at[at]
         )
 
-    for s in range(RING):
-        load(0, s).start()
+    for t in range(min(RING, 4)):
+        load(0, t).start()
     for k0, kc in spans:
         w[k0 : k0 + kc, :] = columns([piece[m, :, k0 : k0 + kc] for m in range(4)])
     for n, (k0, kc) in enumerate(spans):
         cols = slice(k0, k0 + kc)
 
-        def step(s, keep_hi, keep_lo, at, wide_cols):
-            load(n, s).wait()
-            hi, lo = split(buf[lax.rem(4 * n + s, RING), :, :kc])
-            keep_hi[at, wide_cols] = hi
-            keep_lo[at, wide_cols] = lo
-
-            @pl.when(s + RING < 4)
+        @pl.loop(0, 4)
+        def _(t):
+            load(n, t).wait()
+            at = pl.ds(pl.multiple_of(lax.max(t - 1, 0) * share, share), share)
+            hi, lo = split(buf[lax.rem(4 * n + t, RING), :, :kc])
+            his[at, cols] = hi
+            los[at, cols] = lo
+
+            @pl.when(t + RING < 4)
             def _():
-                load(n, s + RING).start()
+                load(n, t + RING).start()
 
             if n + 1 < len(spans):
 
-                @pl.when(s + RING >= 4)
+                @pl.when(t + RING >= 4)
                 def _():
-                    load(n + 1, s + RING - 4).start()
-
-            wide = jnp.dot(keep_hi[at, wide_cols], w[cols, :], preferred_element_type=F32)
-            return fold(wide + jnp.dot(keep_lo[at, wide_cols], w[cols, :], preferred_element_type=F32))
-
-        @pl.loop(0, 3)
-        def _(s):
-            x = step(s, his, los, pl.ds(pl.multiple_of(s * share, share), share), cols)
-            acc[s] = acc[s] + x if n else x
-
-        x = step(3, last.at[0], last.at[1], slice(None), slice(0, kc))
-        outs[0][...] = outs[0][...] + x if n else x
-
-    for s in range(3):
-        outs[3 - s][...] = acc[s]
+                    load(n + 1, t + RING - 4).start()
+
+            wide = jnp.dot(his[at, cols], w[cols, :], preferred_element_type=F32)
+            x = fold(wide + jnp.dot(los[at, cols], w[cols, :], preferred_element_type=F32))
+            acc[t] = acc[t] + x if n else x
+
+    for s in range(4):
+        outs[s][...] = acc[(4 - s) % 4]
+
 
 def near_pass(a, piece):
     rows, cd = a.shape
-    spans = [(k0, min(STEP, cd - k0)) for k0 in range(0, cd, STEP)]
+    spans = ranges(cd, 4)
     kept = jax.ShapeDtypeStruct((rows // 4 * 3, cd), BF16)
     packed = (rows // 8, 128)
     widest = max(kc for _, kc in spans)
@@ -198,8 +193,7 @@
         scratch_shapes=[
             pltpu.VMEM((RING, rows // 4, widest), F32),
             pltpu.VMEM((cd, 128), BF16),
-            pltpu.VMEM((2, rows // 4, widest), BF16),
-            pltpu.VMEM((3, *packed), F32),
+            pltpu.VMEM((4, *packed), F32),
             pltpu.SemaphoreType.DMA((RING,)),
         ],
         compiler_params=params(NEAR_MIB),
@@ -229,36 +223,43 @@
     )(*kept, w)
 
 
-def last_kernel(spans, a, w, out, buf, wide, sem):
-    share = buf.shape[0]
+def last_kernel(parts, a, w, out, buf, his, los, wide, sem):
+    share, kc = buf.shape[1:]
     row = pl.multiple_of(lax.axis_index("ctr") * share, share)
-    loads = [
-        pltpu.make_async_copy(a.at[pl.ds(row, share), pl.ds(*span)], buf.at[:, pl.ds(*span)], sem.at[n])
-        for n, span in enumerate(spans)
-    ]
-    for x in loads:
-        x.start()
-    for n, (x, (k0, kc)) in enumerate(zip(loads, spans)):
-        x.wait()
-        hi, lo = split(buf[:, k0 : k0 + kc])
-        part = jnp.dot(hi, w[k0 : k0 + kc, :], preferred_element_type=F32)
-        part = part + jnp.dot(lo, w[k0 : k0 + kc, :], preferred_element_type=F32)
-        wide[...] = wide[...] + part if n else part
+
+    def load(n):
+        return pltpu.make_async_copy(a.at[pl.ds(row, share), pl.ds(n * kc, kc)], buf.at[n], sem.at[n])
+
+    for n in range(parts):
+        load(n).start()
+    wide[...] = jnp.zeros_like(wide)
+
+    @pl.loop(0, parts)
+    def _(n):
+        load(n).wait()
+        his[...], los[...] = split(buf[n])
+        part = w[pl.ds(pl.multiple_of(n * kc, kc), kc), :]
+        x = jnp.dot(his[...], part, preferred_element_type=F32)
+        wide[...] = wide[...] + (x + jnp.dot(los[...], part, preferred_element_type=F32))
+
     out[...] = fold(wide[...])
 
 
 def last_tile(a, w):
     rows, cd = a.shape
-    spans = ranges(cd, 6)
-    return pl.pallas_call(
-        functools.partial(last_kernel, spans),
+    parts = 5
+    kept = pltpu.VMEM((rows // 4, cd // parts), BF16)
+    return pl.pallas_call(
+        functools.partial(last_kernel, parts),
         out_shape=jax.ShapeDtypeStruct((rows // 8, 128), F32),
         in_specs=[ANY, VMEM],
         out_specs=VMEM,
         scratch_shapes=[
-            pltpu.VMEM((rows // 4, cd), F32),
+            pltpu.VMEM((parts, rows // 4, cd // parts), F32),
+            kept,
+            kept,
             pltpu.VMEM((rows // 4, 128), F32),
-            pltpu.SemaphoreType.DMA((len(spans),)),
+            pltpu.SemaphoreType.DMA((parts,)),
         ],
         compiler_params=params(LAST_MIB),
         cost_estimate=cost(0, 0),
@@ -269,22 +270,23 @@
 def denom_kernel(count, bm, vir, occ, out):
     irrep = bm[lax.axis_index("blk")]
     start = lax.axis_index("ctr") * count
-    vir_at = lax.broadcasted_iota(jnp.int32, (count, vir.shape[1]), 1)
-    rows = start + lax.broadcasted_iota(jnp.int32, (count, vir.shape[1]), 0)
+    vir_at = lax.broadcasted_iota(jnp.int32, (count, vir.shape[0]), 1)
+    rows = start + lax.broadcasted_iota(jnp.int32, (count, vir.shape[0]), 0)
     arow = rows // (VI * VI)
     first = arow * VI + rows // VI % VI
     second = jnp.bitwise_xor(arow, irrep) * VI + rows % VI
-    energy = jnp.broadcast_to(vir[...], vir_at.shape)
+    energy = jnp.broadcast_to(vir[...].reshape(1, -1), vir_at.shape)
     pick = lambda at: jnp.sum(jnp.where(vir_at == at, energy, 0.0), axis=1, keepdims=True)
     upper = pick(first) + pick(second)
-    occ_at = lax.broadcasted_iota(jnp.int32, (occ.shape[0], 128), 0)
-    cols = lax.broadcasted_iota(jnp.int32, (occ.shape[0], 128), 1)
+    cols = lax.broadcasted_iota(jnp.int32, (1, 128), 1)
     orow = cols // (OI * OI)
     hole_one = orow * OI + cols // OI % OI
     hole_two = jnp.bitwise_xor(orow, irrep) * OI + cols % OI
-    level = jnp.broadcast_to(occ[...], occ_at.shape)
-    find = lambda at: jnp.sum(jnp.where(occ_at == at, level, 0.0), axis=0, keepdims=True)
-    lower = find(hole_one) + find(hole_two)
+    one, two = jnp.zeros((1, 128), F32), jnp.zeros((1, 128), F32)
+    for n in range(occ.shape[0]):
+        one = jnp.where(hole_one == n, occ[n], one)
+        two = jnp.where(hole_two == n, occ[n], two)
+    lower = one + two
     out[...] = upper - lower
 
 
@@ -292,12 +294,12 @@
     return pl.pallas_call(
         functools.partial(denom_kernel, count),
         out_shape=jax.ShapeDtypeStruct((count, 128), F32),
-        in_specs=[SMEM, VMEM, VMEM],
+        in_specs=[SMEM, VMEM, SMEM],
         out_specs=VMEM,
         compiler_params=params(8),
         cost_estimate=cost(count * 320 * 8, count * 128 * 4),
         name="denominators",
-    )(blockmap, vir_energy.reshape(1, -1), occ_energy.reshape(-1, 1))
+    )(blockmap, vir_energy, occ_energy)
 
 
 def add_kernel(*refs):
@@ -366,8 +368,8 @@
     to_near, to_far = prep(blockmap, amps)
     near = lax.all_to_all(to_near, "blk", 0, 0, axis_index_groups=[[0, 1, 2, 3], [4, 5, 6, 7]])
     denom = denominators(blockmap, vir_energy, occ_energy, a.shape[0] // 4)
-    far = [swap(after(x, denom), "blk", s) for s, x in zip(FAR, to_far)]
-    kept, sums = near_pass(a, near)
+    far = [swap(x, "blk", s) for s, x in zip(FAR, to_far)]
+    kept, sums = near_pass(a, after(near, denom))
     near_sum = add([sums[0], *[swap(sums[s], "ctr", s) for s in (1, 2, 3)]])
     w = columns_of(far)
     far_sums = {}
@@ -384,7 +386,7 @@
         lax.axis_size("blk") == NIRR
         and lax.axis_size("ctr") == 4
         and rows % 128 == 0
-        and cd % 128 == 0
+        and cd % 640 == 0
         and amplitudes.shape[2] == 16
     )
     return (special if fits else general)(integrals, amplitudes, *rest)

time: 76.7 us -> 72 us (0.939)
  the two profiles are of different devices: /device:TPU:22 before, /device:TPU:0 now
where the time goes in v3:
time: 72 us; the launch traced here: 71.8 us
  Pallas kernels  38.5 us (53%)
  starting transfers between devices  19.1 us (27%)
  waiting for transfers between devices  11.4 us (16%)
  local copies, waits for them, and re-layouts  1.99 us (3%)
  between operations  0.73 us (1%)
    pallas_call x1, Pallas kernels, near_pass(): pl.pallas_call(functools.partial(near_kernel, spans), out_shape=[kept, ke...  17.6 us
    ppermute x10, starting transfers between devices, swap(): return lax.ppermute(x, axis, [(i, i ^ s) for i in range(n)])  14.8 us
    all_to_all x1, waiting for transfers between devices, special(): lax.all_to_all(to_near, 'blk', 0, 0, axis_index_groups=[[0, 1, 2, 3], [4,...  9.68 us
    pallas_call x3, Pallas kernels, far_tile(): pl.pallas_call(functools.partial(far_kernel, s), out_shape=jax.ShapeDtype...  8.68 us
    pallas_call x1, Pallas kernels, last_tile(): pl.pallas_call(functools.partial(last_kernel, parts), out_shape=jax.Shape...  5.24 us
    all_to_all x1, starting transfers between devices, special(): lax.all_to_all(to_near, 'blk', 0, 0, axis_index_groups=[[0, 1, 2, 3], [4,...  4.3 us
    pallas_call x1, Pallas kernels, prep(): pl.pallas_call(prep_kernel, out_shape=[jax.ShapeDtypeStruct((4, *one), F3...  3.4 us
    unnamed x6, local copies, waits for them, and re-layouts  1.99 us
  transfers between devices with their start and end apart: 11, of which 2 were waited for; matrix products, arithmetic and copies ran while one was open for 0% of the time, Pallas kernels for 47%

profile of v3, /device:TPU:0, one launch (start us, length us, event | category | flops | bytes accessed | tf_op | source)
XLA Modules:
  0.0 71.8 jit_solution(13995342961090326595)
XLA Ops:
  0.6 3.4 %prep.1 = (f32[4,16,3200]{2,1,0:T(8,128)}, f32[16,3200]{1,0:T(8,128)}, f32[16,3200]{1,0:T(8,128)}, f32[16,3200]{1,0:T(8,128)}, f32[16,3200]{1,0:T(8,128)}) custom-call(s32[8]{0:T(128)} %bm.3, f32[8,16,3200]{2,1,0:T(8,128)} %bitcast.4), custom_call_target="tpu_custom_call" | custom-call | flops 1 | bytes 1 | tf_op jit(solution)/shard_map/prep/pallas_call | solution.py:82
  4.0 4.3 %all-to-all-start = ((f32[4,16,3200]{2,1,0:T(8,128)}), f32[4,16,3200]{2,1,0:T(8,128)S(1)}, u32[]{:S(2)}, u32[]{:S(2)}) async-start(f32[4,16,3200]{2,1,0:T(8,128)} %get-tuple-element.15), calls=%async_computation | async-start | bytes 1638400 | tf_op jit(solution)/shard_map/all_to_all | solution.py:369
  8.3 3.3 %collective-permute-start.3 = (f32[16,3200]{1,0:T(8,128)}, f32[16,3200]{1,0:T(8,128)S(1)}, u32[]{:S(2)}, u32[]{:S(2)}) collective-permute-start(f32[16,3200]{1,0:T(8,128)} %get-tuple-element.21), channel_id=1, source_target_pairs={{0,16},{4,20},{8,24},{12,28},{16,0},{20,4},{24,8},{28,12},{1,17},{... | collective-permute-start | bytes 614408 | tf_op jit(solution)/shard_map/ppermute | solution.py:352
  11.7 0.1 collective-permute-start.4
  11.7 3.7 %collective-permute-start.5 = (f32[16,3200]{1,0:T(8,128)}, f32[16,3200]{1,0:T(8,128)S(1)}, u32[]{:S(2)}, u32[]{:S(2)}) collective-permute-start(f32[16,3200]{1,0:T(8,128)} %get-tuple-element.23), channel_id=1, source_target_pairs={{0,24},{4,28},{8,16},{12,20},{16,8},{20,12},{24,0},{28,4},{1,25},{... | collective-permute-start | bytes 614408 | tf_op jit(solution)/shard_map/ppermute | solution.py:352
  15.4 0.3 collective-permute-start.6
  15.7 0.7 copy-done
  16.4 0.7 copy-done.1
  17.0 0.7 copy-done.2
  17.7 1.8 %denominators.1.refs_4_ = f32[800,128]{1,0:T(8,128)S(1)} custom-call(s32[8]{0:T(128)S(1)} %copy-done.1, f32[320]{0:T(512)S(1)} %copy-done, f32[32]{0:T(128)S(1)} %copy-done.2), custom_call_target="tpu_custom_call" | custom-call | flops 1 | bytes 1 | tf_op jit(solution)/shard_map/denominators/pallas_call | solution.py:294
  19.4 9.7 %all-to-all-done.piece = f32[4,16,3200]{2,1,0:T(8,128)S(1)} async-done(((f32[4,16,3200]{2,1,0:T(8,128)}), f32[4,16,3200]{2,1,0:T(8,128)S(1)}, u32[]{:S(2)}, u32[]{:S(2)}) %all-to-all-start) | async-done | bytes 819232 | tf_op jit(solution)/shard_map/all_to_all | solution.py:369
  29.1 17.6 %near.1 = (bf16[2400,3200]{1,0:T(8,128)(2,1)S(1)}, bf16[2400,3200]{1,0:T(8,128)(2,1)S(1)}, f32[400,128]{1,0:T(8,128)S(1)}, f32[400,128]{1,0:T(8,128)S(1)}, f32[4...) custom-call(f32[3200,3200]{1,0:T(8,128)} %bitcast.2, f32[4,16,3200]{2,1,0:T(8,128)S(1)} %all-to-all-done.piece), custom_call_target="tpu_custom_call" | custom-call | flops 1 | bytes 1 | tf_op jit(solution)/shard_map/near/pallas_call | solution.py:188
  46.7 2.2 %collective-permute-start = (f32[400,128]{1,0:T(8,128)S(1)}, f32[400,128]{1,0:T(8,128)S(1)}, u32[]{:S(2)}, u32[]{:S(2)}) collective-permute-start(f32[400,128]{1,0:T(8,128)S(1)} %get-tuple-element.18), channel_id=1, source_target_pairs={{0,1},{1,0},{2,3},{3,2},{4,5},{5,4},{6,7},{7,6},{8,9},{9,8},{10,11... | collective-permute-start | bytes 614408 | tf_op jit(solution)/shard_map/ppermute | solution.py:352
  48.9 0.0 collective-permute-done.3.refs_0_
  48.9 0.0 collective-permute-done.4.refs_1_
  48.9 0.0 collective-permute-done.5.refs_2_
  48.9 0.0 collective-permute-done.6.refs_3_
  48.9 0.7 %columns.1.w = bf16[3200,128]{1,0:T(8,128)(2,1)S(1)} custom-call(f32[16,3200]{1,0:T(8,128)S(1)} %collective-permute-done.3.refs_0_, f32[16,3200]{1,0:T(8,128)S(1)} %collective-permute-done.4.refs_1_, f32[16,3200]{1,0:T(8,128)S(1)} %collective-permute-done.5.refs_2_, f32[16,3200]{1,0:T(8,128)S(1)} %collective-permute-done.6.refs_3_), custom_call_target="tpu_custom_call" | custom-call | flops 1 | bytes 1 | tf_op jit(solution)/shard_map/columns/pallas_call | solution.py:118
  49.7 1.6 %collective-permute-start.1 = (f32[400,128]{1,0:T(8,128)S(1)}, f32[400,128]{1,0:T(8,128)S(1)}, u32[]{:S(2)}, u32[]{:S(2)}) collective-permute-start(f32[400,128]{1,0:T(8,128)S(1)} %get-tuple-element.19), channel_id=1, source_target_pairs={{0,2},{1,3},{2,0},{3,1},{4,6},{5,7},{6,4},{7,5},{8,10},{9,11},{10,... | collective-permute-start | bytes 614408 | tf_op jit(solution)/shard_map/ppermute | solution.py:352
  51.2 0.0 collective-permute-start.2
  51.3 2.9 %far.3 = f32[400,128]{1,0:T(8,128)S(1)} custom-call(bf16[2400,3200]{1,0:T(8,128)(2,1)S(1)} %get-tuple-element.25.hi, bf16[2400,3200]{1,0:T(8,128)(2,1)S(1)} %get-tuple-element.26.lo, bf16[3200,128]{1,0:T(8,128)(2,1)S(1)} %columns.1.w), custom_call_target="tpu_custom_call" | custom-call | flops 1 | bytes 1 | tf_op jit(solution)/shard_map/far/pallas_call | solution.py:215
  54.2 3.0 %collective-permute-start.7 = (f32[400,128]{1,0:T(8,128)S(1)}, f32[400,128]{1,0:T(8,128)S(1)}, u32[]{:S(2)}, u32[]{:S(2)}) collective-permute-start(f32[400,128]{1,0:T(8,128)S(1)} %far.3), channel_id=1, source_target_pairs={{0,3},{1,2},{2,1},{3,0},{4,7},{5,6},{6,5},{7,4},{8,11},{9,10},{10,... | collective-permute-start | bytes 614408 | tf_op jit(solution)/shard_map/ppermute | solution.py:352
  57.1 2.9 %far.4 = f32[400,128]{1,0:T(8,128)S(1)} custom-call(bf16[2400,3200]{1,0:T(8,128)(2,1)S(1)} %get-tuple-element.25.hi, bf16[2400,3200]{1,0:T(8,128)(2,1)S(1)} %get-tuple-element.26.lo, bf16[3200,128]{1,0:T(8,128)(2,1)S(1)} %columns.1.w), custom_call_target="tpu_custom_call" | custom-call | flops 1 | bytes 1 | tf_op jit(solution)/shard_map/far/pallas_call | solution.py:215
  60.0 2.9 %far.5 = f32[400,128]{1,0:T(8,128)S(1)} custom-call(bf16[2400,3200]{1,0:T(8,128)(2,1)S(1)} %get-tuple-element.25.hi, bf16[2400,3200]{1,0:T(8,128)(2,1)S(1)} %get-tuple-element.26.lo, bf16[3200,128]{1,0:T(8,128)(2,1)S(1)} %columns.1.w), custom_call_target="tpu_custom_call" | custom-call | flops 1 | bytes 1 | tf_op jit(solution)/shard_map/far/pallas_call | solution.py:215
  62.9 0.6 collective-permute-start.8
  63.5 0.1 collective-permute-start.9
  63.6 1.7 %collective-permute-done.1.refs_2_ = f32[400,128]{1,0:T(8,128)S(1)} collective-permute-done((f32[400,128]{1,0:T(8,128)S(1)}, f32[400,128]{1,0:T(8,128)S(1)}, u32[]{:S(2)}, u32[]{:S(2)}) %collective-permute-start.1) | collective-permute-done | bytes 204832 | tf_op jit(solution)/shard_map/ppermute | solution.py:352
  65.3 0.0 collective-permute-done.2.refs_3_
  65.4 0.0 collective-permute-done.7.refs_3_
  65.4 5.2 %last.1.refs_0_ = f32[400,128]{1,0:T(8,128)S(1)} custom-call(f32[3200,3200]{1,0:T(8,128)} %bitcast.3, bf16[3200,128]{1,0:T(8,128)(2,1)S(1)} %columns.1.w), custom_call_target="tpu_custom_call" | custom-call | flops 1 | bytes 1 | tf_op jit(solution)/shard_map/last/pallas_call | solution.py:252
  70.7 0.0 collective-permute-done.9.refs_2_
  70.7 1.1 %finish.1 = (f32[1,800,128]{2,1,0:T(8,128)}, f32[1,800,128]{2,1,0:T(8,128)}) custom-call(f32[400,128]{1,0:T(8,128)S(1)} %add.1.near, f32[400,128]{1,0:T(8,128)S(1)} %last.1.refs_0_, f32[400,128]{1,0:T(8,128)S(1)} %collective-permute-done.8.refs_1_, f32[400,128]{1,0:T(8,128)S(1)} %collective-permute-done.9.refs_2_, ...), custom_call_target="tpu_custom_call" | custom-call | flops 1 | bytes 1 | tf_op jit(solution)/shard_map/finish/pallas_call | solution.py:339
  (6 shorter events, 0.1 us)
Async XLA Ops:
  4.0 25.1 %all-to-all-start = ((f32[4,16,3200]{2,1,0:T(8,128)}), f32[4,16,3200]{2,1,0:T(8,128)S(1)}, u32[]{:S(2)}, u32[]{:S(2)}) async-start(f32[4,16,3200]{2,1,0:T(8,128)} %get-tuple-element.15), calls=%async_computation | async-start | bytes 1638400 | tf_op jit(solution)/shard_map/all_to_all | solution.py:369
  8.3 40.6 %collective-permute-start.3 = (f32[16,3200]{1,0:T(8,128)}, f32[16,3200]{1,0:T(8,128)S(1)}, u32[]{:S(2)}, u32[]{:S(2)}) collective-permute-start(f32[16,3200]{1,0:T(8,128)} %get-tuple-element.21), channel_id=1, source_target_pairs={{0,16},{4,20},{8,24},{12,28},{16,0},{20,4},{24,8},{28,12},{1,17},{... | collective-permute-start | bytes 614408 | tf_op jit(solution)/shard_map/ppermute | solution.py:352
  11.7 37.2 %collective-permute-start.4 = (f32[16,3200]{1,0:T(8,128)}, f32[16,3200]{1,0:T(8,128)S(1)}, u32[]{:S(2)}, u32[]{:S(2)}) collective-permute-start(f32[16,3200]{1,0:T(8,128)} %get-tuple-element.22), channel_id=1, source_target_pairs={{0,20},{4,16},{8,28},{12,24},{16,4},{20,0},{24,12},{28,8},{1,21},{... | collective-permute-start | bytes 614408 | tf_op jit(solution)/shard_map/ppermute | solution.py:352
  11.7 37.2 %collective-permute-start.5 = (f32[16,3200]{1,0:T(8,128)}, f32[16,3200]{1,0:T(8,128)S(1)}, u32[]{:S(2)}, u32[]{:S(2)}) collective-permute-start(f32[16,3200]{1,0:T(8,128)} %get-tuple-element.23), channel_id=1, source_target_pairs={{0,24},{4,28},{8,16},{12,20},{16,8},{20,12},{24,0},{28,4},{1,25},{... | collective-permute-start | bytes 614408 | tf_op jit(solution)/shard_map/ppermute | solution.py:352
  15.4 33.5 %collective-permute-start.6 = (f32[16,3200]{1,0:T(8,128)}, f32[16,3200]{1,0:T(8,128)S(1)}, u32[]{:S(2)}, u32[]{:S(2)}) collective-permute-start(f32[16,3200]{1,0:T(8,128)} %get-tuple-element.24), channel_id=1, source_target_pairs={{0,28},{4,24},{8,20},{12,16},{16,12},{20,8},{24,4},{28,0},{1,29},{... | collective-permute-start | bytes 614408 | tf_op jit(solution)/shard_map/ppermute | solution.py:352
  15.7 0.7 copy-start
  16.4 0.7 copy-start.1
  17.0 0.7 copy-start.2
  46.7 16.8 %collective-permute-start = (f32[400,128]{1,0:T(8,128)S(1)}, f32[400,128]{1,0:T(8,128)S(1)}, u32[]{:S(2)}, u32[]{:S(2)}) collective-permute-start(f32[400,128]{1,0:T(8,128)S(1)} %get-tuple-element.18), channel_id=1, source_target_pairs={{0,1},{1,0},{2,3},{3,2},{4,5},{5,4},{6,7},{7,6},{8,9},{9,8},{10,11... | collective-permute-start | bytes 614408 | tf_op jit(solution)/shard_map/ppermute | solution.py:352
  49.7 15.7 %collective-permute-start.1 = (f32[400,128]{1,0:T(8,128)S(1)}, f32[400,128]{1,0:T(8,128)S(1)}, u32[]{:S(2)}, u32[]{:S(2)}) collective-permute-start(f32[400,128]{1,0:T(8,128)S(1)} %get-tuple-element.19), channel_id=1, source_target_pairs={{0,2},{1,3},{2,0},{3,1},{4,6},{5,7},{6,4},{7,5},{8,10},{9,11},{10,... | collective-permute-start | bytes 614408 | tf_op jit(solution)/shard_map/ppermute | solution.py:352
  51.2 14.1 %collective-permute-start.2 = (f32[400,128]{1,0:T(8,128)S(1)}, f32[400,128]{1,0:T(8,128)S(1)}, u32[]{:S(2)}, u32[]{:S(2)}) collective-permute-start(f32[400,128]{1,0:T(8,128)S(1)} %get-tuple-element.20), channel_id=1, source_target_pairs={{0,3},{1,2},{2,1},{3,0},{4,7},{5,6},{6,5},{7,4},{8,11},{9,10},{10,... | collective-permute-start | bytes 614408 | tf_op jit(solution)/shard_map/ppermute | solution.py:352
  54.2 11.2 %collective-permute-start.7 = (f32[400,128]{1,0:T(8,128)S(1)}, f32[400,128]{1,0:T(8,128)S(1)}, u32[]{:S(2)}, u32[]{:S(2)}) collective-permute-start(f32[400,128]{1,0:T(8,128)S(1)} %far.3), channel_id=1, source_target_pairs={{0,3},{1,2},{2,1},{3,0},{4,7},{5,6},{6,5},{7,4},{8,11},{9,10},{10,... | collective-permute-start | bytes 614408 | tf_op jit(solution)/shard_map/ppermute | solution.py:352
  62.9 7.7 %collective-permute-start.8 = (f32[400,128]{1,0:T(8,128)S(1)}, f32[400,128]{1,0:T(8,128)S(1)}, u32[]{:S(2)}, u32[]{:S(2)}) collective-permute-start(f32[400,128]{1,0:T(8,128)S(1)} %far.5), channel_id=1, source_target_pairs={{0,1},{1,0},{2,3},{3,2},{4,5},{5,4},{6,7},{7,6},{8,9},{9,8},{10,11... | collective-permute-start | bytes 614408 | tf_op jit(solution)/shard_map/ppermute | solution.py:352
  63.5 7.1 %collective-permute-start.9 = (f32[400,128]{1,0:T(8,128)S(1)}, f32[400,128]{1,0:T(8,128)S(1)}, u32[]{:S(2)}, u32[]{:S(2)}) collective-permute-start(f32[400,128]{1,0:T(8,128)S(1)} %far.4), channel_id=1, source_target_pairs={{0,2},{1,3},{2,0},{3,1},{4,6},{5,7},{6,4},{7,5},{8,10},{9,11},{10,... | collective-permute-start | bytes 614408 | tf_op jit(solution)/shard_map/ppermute | solution.py:352

commit v4 on v3

--- a/solution.py
+++ b/solution.py
@@ -370,7 +370,7 @@
     denom = denominators(blockmap, vir_energy, occ_energy, a.shape[0] // 4)
     far = [swap(x, "blk", s) for s, x in zip(FAR, to_far)]
     kept, sums = near_pass(a, after(near, denom))
-    near_sum = add([sums[0], *[swap(sums[s], "ctr", s) for s in (1, 2, 3)]])
+    near_sum = add([sums[0], *[swap(sums[s], "ctr", s) for s in (3, 1, 2)]])
     w = columns_of(far)
     far_sums = {}
     for s in (3, 1, 2):

time: 72 us -> 70.7 us (0.982)
  waiting for transfers between devices: 11.4 us -> 10.1 us
    ppermute x10, waiting for transfers between devices: 1.76 us -> 0.38 us  [swap(): return lax.ppermute(x, axis, [(i, i ^ s) for i in range(n)])]
  transfers between devices with their start and end apart: 11 -> 11, of which waited for: 2 -> 2; matrix products, arithmetic and copies ran while one was open for 0% -> 0% of each run, Pallas kernels for 47% -> 48%
where the time goes in v4:
time: 70.7 us; the launch traced here: 70.4 us
  Pallas kernels  38.5 us (54%)
  starting transfers between devices  19.1 us (27%)
  waiting for transfers between devices  10.1 us (14%)
  local copies, waits for them, and re-layouts  1.99 us (3%)
  between operations  0.73 us (1%)
    pallas_call x1, Pallas kernels, near_pass(): pl.pallas_call(functools.partial(near_kernel, spans), out_shape=[kept, ke...  17.6 us
    ppermute x10, starting transfers between devices, swap(): return lax.ppermute(x, axis, [(i, i ^ s) for i in range(n)])  14.8 us
    all_to_all x1, waiting for transfers between devices, special(): lax.all_to_all(to_near, 'blk', 0, 0, axis_index_groups=[[0, 1, 2, 3], [4,...  9.68 us
    pallas_call x3, Pallas kernels, far_tile(): pl.pallas_call(functools.partial(far_kernel, s), out_shape=jax.ShapeDtype...  8.68 us
    pallas_call x1, Pallas kernels, last_tile(): pl.pallas_call(functools.partial(last_kernel, parts), out_shape=jax.Shape...  5.24 us
    all_to_all x1, starting transfers between devices, special(): lax.all_to_all(to_near, 'blk', 0, 0, axis_index_groups=[[0, 1, 2, 3], [4,...  4.3 us
    pallas_call x1, Pallas kernels, prep(): pl.pallas_call(prep_kernel, out_shape=[jax.ShapeDtypeStruct((4, *one), F3...  3.4 us
    unnamed x6, local copies, waits for them, and re-layouts  1.99 us
  transfers between devices with their start and end apart: 11, of which 2 were waited for; matrix products, arithmetic and copies ran while one was open for 0% of the time, Pallas kernels for 48%

profile of v4, /device:TPU:0, one launch (start us, length us, event | category | flops | bytes accessed | tf_op | source)
XLA Modules:
  0.0 70.4 jit_solution(11765327089764919238)
XLA Ops:
  0.6 3.4 %prep.1 = (f32[4,16,3200]{2,1,0:T(8,128)}, f32[16,3200]{1,0:T(8,128)}, f32[16,3200]{1,0:T(8,128)}, f32[16,3200]{1,0:T(8,128)}, f32[16,3200]{1,0:T(8,128)}) custom-call(s32[8]{0:T(128)} %bm.3, f32[8,16,3200]{2,1,0:T(8,128)} %bitcast.4), custom_call_target="tpu_custom_call" | custom-call | flops 1 | bytes 1 | tf_op jit(solution)/shard_map/prep/pallas_call | solution.py:82
  4.0 4.3 %all-to-all-start = ((f32[4,16,3200]{2,1,0:T(8,128)}), f32[4,16,3200]{2,1,0:T(8,128)S(1)}, u32[]{:S(2)}, u32[]{:S(2)}) async-start(f32[4,16,3200]{2,1,0:T(8,128)} %get-tuple-element.15), calls=%async_computation | async-start | bytes 1638400 | tf_op jit(solution)/shard_map/all_to_all | solution.py:369
  8.3 3.3 %collective-permute-start.3 = (f32[16,3200]{1,0:T(8,128)}, f32[16,3200]{1,0:T(8,128)S(1)}, u32[]{:S(2)}, u32[]{:S(2)}) collective-permute-start(f32[16,3200]{1,0:T(8,128)} %get-tuple-element.21), channel_id=1, source_target_pairs={{0,16},{4,20},{8,24},{12,28},{16,0},{20,4},{24,8},{28,12},{1,17},{... | collective-permute-start | bytes 614408 | tf_op jit(solution)/shard_map/ppermute | solution.py:352
  11.7 0.1 collective-permute-start.4
  11.7 3.7 %collective-permute-start.5 = (f32[16,3200]{1,0:T(8,128)}, f32[16,3200]{1,0:T(8,128)S(1)}, u32[]{:S(2)}, u32[]{:S(2)}) collective-permute-start(f32[16,3200]{1,0:T(8,128)} %get-tuple-element.23), channel_id=1, source_target_pairs={{0,24},{4,28},{8,16},{12,20},{16,8},{20,12},{24,0},{28,4},{1,25},{... | collective-permute-start | bytes 614408 | tf_op jit(solution)/shard_map/ppermute | solution.py:352
  15.4 0.3 collective-permute-start.6
  15.7 0.7 copy-done
  16.4 0.7 copy-done.1
  17.0 0.7 copy-done.2
  17.7 1.8 %denominators.1.refs_4_ = f32[800,128]{1,0:T(8,128)S(1)} custom-call(s32[8]{0:T(128)S(1)} %copy-done.1, f32[320]{0:T(512)S(1)} %copy-done, f32[32]{0:T(128)S(1)} %copy-done.2), custom_call_target="tpu_custom_call" | custom-call | flops 1 | bytes 1 | tf_op jit(solution)/shard_map/denominators/pallas_call | solution.py:294
  19.4 9.7 %all-to-all-done.piece = f32[4,16,3200]{2,1,0:T(8,128)S(1)} async-done(((f32[4,16,3200]{2,1,0:T(8,128)}), f32[4,16,3200]{2,1,0:T(8,128)S(1)}, u32[]{:S(2)}, u32[]{:S(2)}) %all-to-all-start) | async-done | bytes 819232 | tf_op jit(solution)/shard_map/all_to_all | solution.py:369
  29.1 17.6 %near.1 = (bf16[2400,3200]{1,0:T(8,128)(2,1)S(1)}, bf16[2400,3200]{1,0:T(8,128)(2,1)S(1)}, f32[400,128]{1,0:T(8,128)S(1)}, f32[400,128]{1,0:T(8,128)S(1)}, f32[4...) custom-call(f32[3200,3200]{1,0:T(8,128)} %bitcast.2, f32[4,16,3200]{2,1,0:T(8,128)S(1)} %all-to-all-done.piece), custom_call_target="tpu_custom_call" | custom-call | flops 1 | bytes 1 | tf_op jit(solution)/shard_map/near/pallas_call | solution.py:188
  46.7 3.1 %collective-permute-start = (f32[400,128]{1,0:T(8,128)S(1)}, f32[400,128]{1,0:T(8,128)S(1)}, u32[]{:S(2)}, u32[]{:S(2)}) collective-permute-start(f32[400,128]{1,0:T(8,128)S(1)} %get-tuple-element.18), channel_id=1, source_target_pairs={{0,3},{1,2},{2,1},{3,0},{4,7},{5,6},{6,5},{7,4},{8,11},{9,10},{10,... | collective-permute-start | bytes 614408 | tf_op jit(solution)/shard_map/ppermute | solution.py:352
  49.8 0.0 collective-permute-done.3.refs_0_
  49.9 0.0 collective-permute-done.4.refs_1_
  49.9 0.0 collective-permute-done.6.refs_3_
  49.9 0.7 %columns.1.w = bf16[3200,128]{1,0:T(8,128)(2,1)S(1)} custom-call(f32[16,3200]{1,0:T(8,128)S(1)} %collective-permute-done.3.refs_0_, f32[16,3200]{1,0:T(8,128)S(1)} %collective-permute-done.4.refs_1_, f32[16,3200]{1,0:T(8,128)S(1)} %collective-permute-done.5.refs_2_, f32[16,3200]{1,0:T(8,128)S(1)} %collective-permute-done.6.refs_3_), custom_call_target="tpu_custom_call" | custom-call | flops 1 | bytes 1 | tf_op jit(solution)/shard_map/columns/pallas_call | solution.py:118
  50.6 0.6 collective-permute-start.1
  51.2 0.1 collective-permute-start.2
  51.3 2.9 %far.3 = f32[400,128]{1,0:T(8,128)S(1)} custom-call(bf16[2400,3200]{1,0:T(8,128)(2,1)S(1)} %get-tuple-element.25.hi, bf16[2400,3200]{1,0:T(8,128)(2,1)S(1)} %get-tuple-element.26.lo, bf16[3200,128]{1,0:T(8,128)(2,1)S(1)} %columns.1.w), custom_call_target="tpu_custom_call" | custom-call | flops 1 | bytes 1 | tf_op jit(solution)/shard_map/far/pallas_call | solution.py:215
  54.2 3.0 %collective-permute-start.7 = (f32[400,128]{1,0:T(8,128)S(1)}, f32[400,128]{1,0:T(8,128)S(1)}, u32[]{:S(2)}, u32[]{:S(2)}) collective-permute-start(f32[400,128]{1,0:T(8,128)S(1)} %far.3), channel_id=1, source_target_pairs={{0,3},{1,2},{2,1},{3,0},{4,7},{5,6},{6,5},{7,4},{8,11},{9,10},{10,... | collective-permute-start | bytes 614408 | tf_op jit(solution)/shard_map/ppermute | solution.py:352
  57.1 2.9 %far.4 = f32[400,128]{1,0:T(8,128)S(1)} custom-call(bf16[2400,3200]{1,0:T(8,128)(2,1)S(1)} %get-tuple-element.25.hi, bf16[2400,3200]{1,0:T(8,128)(2,1)S(1)} %get-tuple-element.26.lo, bf16[3200,128]{1,0:T(8,128)(2,1)S(1)} %columns.1.w), custom_call_target="tpu_custom_call" | custom-call | flops 1 | bytes 1 | tf_op jit(solution)/shard_map/far/pallas_call | solution.py:215
  60.0 2.9 %far.5 = f32[400,128]{1,0:T(8,128)S(1)} custom-call(bf16[2400,3200]{1,0:T(8,128)(2,1)S(1)} %get-tuple-element.25.hi, bf16[2400,3200]{1,0:T(8,128)(2,1)S(1)} %get-tuple-element.26.lo, bf16[3200,128]{1,0:T(8,128)(2,1)S(1)} %columns.1.w), custom_call_target="tpu_custom_call" | custom-call | flops 1 | bytes 1 | tf_op jit(solution)/shard_map/far/pallas_call | solution.py:215
  62.9 0.6 collective-permute-start.8
  63.5 0.1 collective-permute-start.9
  63.6 0.0 collective-permute-done.1.refs_2_
  63.6 0.0 collective-permute-done.2.refs_3_
  63.7 0.0 collective-permute-done.7.refs_3_
  63.7 5.2 %last.1.refs_0_ = f32[400,128]{1,0:T(8,128)S(1)} custom-call(f32[3200,3200]{1,0:T(8,128)} %bitcast.3, bf16[3200,128]{1,0:T(8,128)(2,1)S(1)} %columns.1.w), custom_call_target="tpu_custom_call" | custom-call | flops 1 | bytes 1 | tf_op jit(solution)/shard_map/last/pallas_call | solution.py:252
  68.9 0.0 collective-permute-done.8.refs_1_
  68.9 0.4 collective-permute-done.9.refs_2_
  69.3 1.1 %finish.1 = (f32[1,800,128]{2,1,0:T(8,128)}, f32[1,800,128]{2,1,0:T(8,128)}) custom-call(f32[400,128]{1,0:T(8,128)S(1)} %add.1.near, f32[400,128]{1,0:T(8,128)S(1)} %last.1.refs_0_, f32[400,128]{1,0:T(8,128)S(1)} %collective-permute-done.8.refs_1_, f32[400,128]{1,0:T(8,128)S(1)} %collective-permute-done.9.refs_2_, ...), custom_call_target="tpu_custom_call" | custom-call | flops 1 | bytes 1 | tf_op jit(solution)/shard_map/finish/pallas_call | solution.py:339
  (6 shorter events, 0.1 us)
Async XLA Ops:
  4.0 25.1 %all-to-all-start = ((f32[4,16,3200]{2,1,0:T(8,128)}), f32[4,16,3200]{2,1,0:T(8,128)S(1)}, u32[]{:S(2)}, u32[]{:S(2)}) async-start(f32[4,16,3200]{2,1,0:T(8,128)} %get-tuple-element.15), calls=%async_computation | async-start | bytes 1638400 | tf_op jit(solution)/shard_map/all_to_all | solution.py:369
  8.3 41.5 %collective-permute-start.3 = (f32[16,3200]{1,0:T(8,128)}, f32[16,3200]{1,0:T(8,128)S(1)}, u32[]{:S(2)}, u32[]{:S(2)}) collective-permute-start(f32[16,3200]{1,0:T(8,128)} %get-tuple-element.21), channel_id=1, source_target_pairs={{0,16},{4,20},{8,24},{12,28},{16,0},{20,4},{24,8},{28,12},{1,17},{... | collective-permute-start | bytes 614408 | tf_op jit(solution)/shard_map/ppermute | solution.py:352
  11.7 38.2 %collective-permute-start.4 = (f32[16,3200]{1,0:T(8,128)}, f32[16,3200]{1,0:T(8,128)S(1)}, u32[]{:S(2)}, u32[]{:S(2)}) collective-permute-start(f32[16,3200]{1,0:T(8,128)} %get-tuple-element.22), channel_id=1, source_target_pairs={{0,20},{4,16},{8,28},{12,24},{16,4},{20,0},{24,12},{28,8},{1,21},{... | collective-permute-start | bytes 614408 | tf_op jit(solution)/shard_map/ppermute | solution.py:352
  11.7 38.1 %collective-permute-start.5 = (f32[16,3200]{1,0:T(8,128)}, f32[16,3200]{1,0:T(8,128)S(1)}, u32[]{:S(2)}, u32[]{:S(2)}) collective-permute-start(f32[16,3200]{1,0:T(8,128)} %get-tuple-element.23), channel_id=1, source_target_pairs={{0,24},{4,28},{8,16},{12,20},{16,8},{20,12},{24,0},{28,4},{1,25},{... | collective-permute-start | bytes 614408 | tf_op jit(solution)/shard_map/ppermute | solution.py:352
  15.4 34.4 %collective-permute-start.6 = (f32[16,3200]{1,0:T(8,128)}, f32[16,3200]{1,0:T(8,128)S(1)}, u32[]{:S(2)}, u32[]{:S(2)}) collective-permute-start(f32[16,3200]{1,0:T(8,128)} %get-tuple-element.24), channel_id=1, source_target_pairs={{0,28},{4,24},{8,20},{12,16},{16,12},{20,8},{24,4},{28,0},{1,29},{... | collective-permute-start | bytes 614408 | tf_op jit(solution)/shard_map/ppermute | solution.py:352
  15.7 0.7 copy-start
  16.4 0.7 copy-start.1
  17.0 0.7 copy-start.2
  46.7 16.8 %collective-permute-start = (f32[400,128]{1,0:T(8,128)S(1)}, f32[400,128]{1,0:T(8,128)S(1)}, u32[]{:S(2)}, u32[]{:S(2)}) collective-permute-start(f32[400,128]{1,0:T(8,128)S(1)} %get-tuple-element.18), channel_id=1, source_target_pairs={{0,3},{1,2},{2,1},{3,0},{4,7},{5,6},{6,5},{7,4},{8,11},{9,10},{10,... | collective-permute-start | bytes 614408 | tf_op jit(solution)/shard_map/ppermute | solution.py:352
  50.6 13.0 %collective-permute-start.1 = (f32[400,128]{1,0:T(8,128)S(1)}, f32[400,128]{1,0:T(8,128)S(1)}, u32[]{:S(2)}, u32[]{:S(2)}) collective-permute-start(f32[400,128]{1,0:T(8,128)S(1)} %get-tuple-element.19), channel_id=1, source_target_pairs={{0,1},{1,0},{2,3},{3,2},{4,5},{5,4},{6,7},{7,6},{8,9},{9,8},{10,11... | collective-permute-start | bytes 614408 | tf_op jit(solution)/shard_map/ppermute | solution.py:352
  51.2 12.4 %collective-permute-start.2 = (f32[400,128]{1,0:T(8,128)S(1)}, f32[400,128]{1,0:T(8,128)S(1)}, u32[]{:S(2)}, u32[]{:S(2)}) collective-permute-start(f32[400,128]{1,0:T(8,128)S(1)} %get-tuple-element.20), channel_id=1, source_target_pairs={{0,2},{1,3},{2,0},{3,1},{4,6},{5,7},{6,4},{7,5},{8,10},{9,11},{10,... | collective-permute-start | bytes 614408 | tf_op jit(solution)/shard_map/ppermute | solution.py:352
  54.2 9.5 %collective-permute-start.7 = (f32[400,128]{1,0:T(8,128)S(1)}, f32[400,128]{1,0:T(8,128)S(1)}, u32[]{:S(2)}, u32[]{:S(2)}) collective-permute-start(f32[400,128]{1,0:T(8,128)S(1)} %far.3), channel_id=1, source_target_pairs={{0,3},{1,2},{2,1},{3,0},{4,7},{5,6},{6,5},{7,4},{8,11},{9,10},{10,... | collective-permute-start | bytes 614408 | tf_op jit(solution)/shard_map/ppermute | solution.py:352
  62.9 6.0 %collective-permute-start.8 = (f32[400,128]{1,0:T(8,128)S(1)}, f32[400,128]{1,0:T(8,128)S(1)}, u32[]{:S(2)}, u32[]{:S(2)}) collective-permute-start(f32[400,128]{1,0:T(8,128)S(1)} %far.5), channel_id=1, source_target_pairs={{0,1},{1,0},{2,3},{3,2},{4,5},{5,4},{6,7},{7,6},{8,9},{9,8},{10,11... | collective-permute-start | bytes 614408 | tf_op jit(solution)/shard_map/ppermute | solution.py:352
  63.5 5.8 %collective-permute-start.9 = (f32[400,128]{1,0:T(8,128)S(1)}, f32[400,128]{1,0:T(8,128)S(1)}, u32[]{:S(2)}, u32[]{:S(2)}) collective-permute-start(f32[400,128]{1,0:T(8,128)S(1)} %far.4), channel_id=1, source_target_pairs={{0,2},{1,3},{2,0},{3,1},{4,6},{5,7},{6,4},{7,5},{8,10},{9,11},{10,... | collective-permute-start | bytes 614408 | tf_op jit(solution)/shard_map/ppermute | solution.py:352
